TPU v7x, 32 devices: a whole 2x2x4 slice. The times are simulated.
32 devices in a mesh: grp: 4 (over z), col: 8 (over y, x, core).
Axes of the slice: x: 2, y: 2, z: 4, core: 2. Of those that a mesh axis runs over, the one named last changes fastest.
Arguments:
- descriptors: bfloat16 [10, 32, 32, 1024], P(None, None, 'grp', 'col'), may hold values from -6 to 6
- solid_temp: float32 [32, 32, 1024], P(None, 'grp', 'col'), may hold values from -6 to 6
- fluid_temp: float32 [32, 32, 1024], P(None, 'grp', 'col'), may hold values from -6 to 6
- material: int32 [32, 32, 1024], P(None, 'grp', 'col'), may hold values from 0 to 3
- fixed_mask: int32 [32, 32, 1024], P(None, 'grp', 'col'), may hold values 0 or 1
- solid_cond: float32 [4], replicated, may hold values from 0.3 to 1.5
- fluid_cond: float32 [4], replicated, may hold values from 0.3 to 1.5
- w_in: bfloat16 [12, 64], replicated, may hold values from -1.75 to 1.75
- b_in: float32 [64], replicated, may hold values from -3 to 3
- w_mid: bfloat16 [64, 64], replicated, may hold values from -0.75 to 0.75
- b_mid: float32 [64], replicated, may hold values from -3 to 3
- w_out: bfloat16 [64, 2], replicated, may hold values from -0.75 to 0.75
- b_out: float32 [2], replicated, may hold values from -3 to 3
- solid_cot: float32 [32, 32, 1024], P(None, 'grp', 'col'), may hold values from -18 to 18
- fluid_cot: float32 [32, 32, 1024], P(None, 'grp', 'col'), may hold values from -18 to 18
Outputs:
- adj_solid: float32 [32, 32, 1024], P(None, 'grp', 'col')
- adj_fluid: float32 [32, 32, 1024], P(None, 'grp', 'col')
- grad_w_in: float32 [12, 64], replicated
- grad_b_in: float32 [64], replicated
- grad_w_mid: float32 [64, 64], replicated
- grad_b_mid: float32 [64], replicated
- grad_w_out: float32 [64, 2], replicated
- grad_b_out: float32 [2], replicated
All inputs are finite; a program needn't handle non-finite values. No bound on the sum of `fixed_mask` on one device may be relied on, other than what follows from the above.
Results may differ from a plain program's by a relative error of at most 0.01.
The roundings to bfloat16 on the way count: a program that leaves them out, or rounds other values in their place, can miss the bound.
Values sent between devices are 32-bit elements; how exact they have to be, the bound alone decides.
A program may use at most 64 MiB of HBM per device.

v0:
```python
import math

import jax
import jax.numpy as jnp
from jax import lax
from jax.sharding import PartitionSpec as P

time_step = 0.15
loss_gain = 16.0


def padded_2(block, sides, width):
    for axis, dim in sides:
        count = lax.axis_size(axis)
        forward = [(i, i + 1) for i in range(count - 1)]
        backward = [(target, source) for source, target in forward]
        low = lax.ppermute(
            lax.slice_in_dim(block, block.shape[dim] - width, None, axis=dim), axis, forward
        )
        high = lax.ppermute(lax.slice_in_dim(block, 0, width, axis=dim), axis, backward)
        block = jnp.concatenate([low, block, high], axis=dim)
    return block


def material_lookup(material, lookup_table):
    summed = jnp.zeros(material.shape, jnp.float32)
    for material_kind in range(lookup_table.shape[0]):
        summed = summed + jnp.where(material == material_kind, lookup_table[material_kind], 0.0)
    return summed


def neighbour_sum(padded, values_field):
    return (
        padded[:, :, 2:, 1:-1]
        + padded[:, :, :-2, 1:-1]
        + padded[:, :, 1:-1, 2:]
        + padded[:, :, 1:-1, :-2]
        - 4.0 * values_field
    )


def network(features, w_in, b_in, w_mid, b_mid, w_out, b_out):
    hidden_one = jnp.tanh(
        jnp.dot(w_in.T, features, preferred_element_type=jnp.float32) + b_in[:, None]
    ).astype(jnp.bfloat16)
    hidden_two = jnp.tanh(
        jnp.dot(w_mid.T, hidden_one, preferred_element_type=jnp.float32) + b_mid[:, None]
    ).astype(jnp.bfloat16)
    logits = jnp.dot(w_out.T, hidden_two, preferred_element_type=jnp.float32) + b_out[:, None]
    return (hidden_one, hidden_two, logits)


def coupling_terms(logits):
    transfer_coef = jax.nn.softplus(logits[0])
    area_coef = jax.nn.softplus(logits[1])
    return (transfer_coef * area_coef, transfer_coef, area_coef)


def backprop(features, hidden_one, hidden_two, logits, d_coupling, w_in, w_mid, w_out):
    coupling, transfer_coef, area_coef = coupling_terms(logits)
    d_logits = jnp.stack(
        [
            d_coupling * area_coef * jax.nn.sigmoid(logits[0]),
            d_coupling * transfer_coef * jax.nn.sigmoid(logits[1]),
        ]
    ).astype(jnp.bfloat16)
    d_hidden_two = (
        jnp.dot(w_out, d_logits, preferred_element_type=jnp.float32)
        * (1.0 - jnp.square(hidden_two.astype(jnp.float32)))
    ).astype(jnp.bfloat16)
    d_hidden_one = (
        jnp.dot(w_mid, d_hidden_two, preferred_element_type=jnp.float32)
        * (1.0 - jnp.square(hidden_one.astype(jnp.float32)))
    ).astype(jnp.bfloat16)
    d_features = jnp.dot(
        w_in[w_in.shape[0] - 2 :], d_hidden_one, preferred_element_type=jnp.float32
    )
    gradients = (
        jnp.dot(features, d_hidden_one.T, preferred_element_type=jnp.float32),
        jnp.sum(d_hidden_one.astype(jnp.float32), axis=1),
        jnp.dot(hidden_one, d_hidden_two.T, preferred_element_type=jnp.float32),
        jnp.sum(d_hidden_two.astype(jnp.float32), axis=1),
        jnp.dot(hidden_two, d_logits.T, preferred_element_type=jnp.float32),
        jnp.sum(d_logits.astype(jnp.float32), axis=1),
    )
    return (coupling, d_features, gradients)


def build_features(desc_line, solid_line, fluid_line):
    cells = solid_line.size
    return jnp.concatenate(
        [
            desc_line.reshape(desc_line.shape[0], cells),
            solid_line.reshape(1, cells).astype(jnp.bfloat16),
            fluid_line.reshape(1, cells).astype(jnp.bfloat16),
        ],
        axis=0,
    )


def forward_coupling(descriptors, solid, fluid, weights):

    def forward_one_line(line_index):
        desc_line = lax.dynamic_index_in_dim(descriptors, line_index, 1, keepdims=False)
        solid_line = lax.dynamic_index_in_dim(solid, line_index, 0, keepdims=False)
        fluid_line = lax.dynamic_index_in_dim(fluid, line_index, 0, keepdims=False)
        features = build_features(desc_line, solid_line, fluid_line)
        logits = network(features, *weights)[2]
        return coupling_terms(logits)[0].reshape(solid_line.shape)

    return lax.map(forward_one_line, jnp.arange(solid.shape[0], dtype=jnp.int32))


def backward_lines(descriptors, solid, fluid, d_coupling, weights, running):
    w_in, b_in, w_mid, b_mid, w_out, b_out = weights

    def backward_one_line(running, line_index):
        desc_line = lax.dynamic_index_in_dim(descriptors, line_index, 1, keepdims=False)
        solid_line = lax.dynamic_index_in_dim(solid, line_index, 0, keepdims=False)
        fluid_line = lax.dynamic_index_in_dim(fluid, line_index, 0, keepdims=False)
        d_line = lax.dynamic_index_in_dim(d_coupling, line_index, 0, keepdims=False)
        features = build_features(desc_line, solid_line, fluid_line)
        hidden_one, hidden_two, logits = network(features, *weights)
        coupling, d_features, gradients = backprop(
            features, hidden_one, hidden_two, logits, d_line.reshape(-1), w_in, w_mid, w_out
        )
        running = tuple((left + right for left, right in zip(running, gradients)))
        line_shape = solid_line.shape
        return (running, (coupling.reshape(line_shape), d_features.reshape((2,) + line_shape)))

    running, (coupling, d_features) = lax.scan(
        backward_one_line, running, jnp.arange(solid.shape[0], dtype=jnp.int32)
    )
    return (running, coupling, jnp.moveaxis(d_features, 1, 0))


def advance(state, state_padded, conduct, free_cell, first_coupling):
    coupled = first_coupling * (state[1] - state[0])
    return state + time_step * free_cell * (
        conduct * neighbour_sum(state_padded, state) + jnp.stack([coupled, -coupled])
    )


def shards(
    descriptors,
    solid_temp,
    fluid_temp,
    material,
    fixed_mask,
    solid_cond,
    fluid_cond,
    w_in,
    b_in,
    w_mid,
    b_mid,
    w_out,
    b_out,
    solid_cot,
    fluid_cot,
):
    weights = (w_in, b_in, w_mid, b_mid, w_out, b_out)
    conduct = jnp.stack(
        [material_lookup(material, solid_cond), material_lookup(material, fluid_cond)]
    )
    free_cell = 1.0 - fixed_mask.astype(jnp.float32)
    state = jnp.stack([solid_temp, fluid_temp])
    first_coupling = forward_coupling(descriptors, state[0], state[1], weights)
    cotangent = jnp.stack([solid_cot, fluid_cot])
    upstream = time_step * free_cell * cotangent
    pushed = conduct * upstream
    padded_all = padded_2(jnp.concatenate([state, pushed]), (("grp", 2), ("col", 3)), 1)
    later = advance(state, padded_all[:2], conduct, free_cell, first_coupling)
    pushed_rim = padded_all[2:]
    running = (
        jnp.zeros(w_in.shape, jnp.float32),
        jnp.zeros(b_in.shape, jnp.float32),
        jnp.zeros(w_mid.shape, jnp.float32),
        jnp.zeros(b_mid.shape, jnp.float32),
        jnp.zeros(w_out.shape, jnp.float32),
        jnp.zeros(b_out.shape, jnp.float32),
    )
    d_coupling = (later[1] - later[0]) * (upstream[0] - upstream[1])
    running, coupling, d_features = backward_lines(
        descriptors, later[0], later[1], d_coupling, weights, running
    )
    swing_term = coupling * (upstream[1] - upstream[0])
    cotangent = (
        cotangent
        + neighbour_sum(pushed_rim, pushed)
        + jnp.stack([swing_term, -swing_term])
        + d_features
    )
    upstream = time_step * free_cell * cotangent
    pushed = conduct * upstream
    pushed_rim = padded_2(pushed, (("grp", 2), ("col", 3)), 1)
    d_coupling = (state[1] - state[0]) * (upstream[0] - upstream[1])
    running, coupling, d_features = backward_lines(
        descriptors, state[0], state[1], d_coupling, weights, running
    )
    swing_term = coupling * (upstream[1] - upstream[0])
    cotangent = (
        cotangent
        + neighbour_sum(pushed_rim, pushed)
        + jnp.stack([swing_term, -swing_term])
        + d_features
    )
    summed = lax.psum(
        (running[0], running[1], running[2], running[3], running[4], running[5]), ("grp", "col")
    )
    cell_count = solid_temp.size * lax.axis_size("grp") * lax.axis_size("col")
    scale = loss_gain / math.sqrt(cell_count)
    return (
        cotangent[0],
        cotangent[1],
        summed[0] * scale,
        summed[1] * scale,
        summed[2] * scale,
        summed[3] * scale,
        summed[4] * scale,
        summed[5] * scale,
    )


def solution(mesh):
    placed = (
        P(None, None, "grp", "col"),
        P(None, "grp", "col"),
        P(None, "grp", "col"),
        P(None, "grp", "col"),
        P(None, "grp", "col"),
        P(),
        P(),
        P(),
        P(),
        P(),
        P(),
        P(),
        P(),
        P(None, "grp", "col"),
        P(None, "grp", "col"),
    )
    return jax.shard_map(
        shards,
        mesh=mesh,
        in_specs=placed,
        out_specs=(P(None, "grp", "col"), P(None, "grp", "col"), P(), P(), P(), P(), P(), P()),
        check_vma=False,
    )
```

profile of v0, /device:TPU:4, one launch (start us, length us, event | category | flops | bytes accessed | tf_op | source)
XLA Modules:
  0.0 759.2 jit_solution(7168458463491345305)
XLA Ops:
  0.6 1.4 fusion.97
  2.6 3.7 add_bitcast_fusion.1
  6.3 2.7 add_bitcast_fusion
  10.2 1.3 collective-permute-start
  11.5 4.5 collective-permute-start.1
  16.8 125.1 %while.59 = (s32[]{:T(128)}, f32[32,8,128]{2,1,0:T(8,128)S(1)}, s32[32]{0:T(128)S(1)}, bf16[10,32,8,128]{3,2,1,0:T(8,128)(2,1)}, bf16[32,8,128]{2,1,0:T(8,128)(2...) while((s32[]{:T(128)}, f32[32,8,128]{2,1,0:T(8,128)S(1)}, ...), condition=%wide.region_1.2_spmd, body=%wide.region_0.1_spmd.sunk | while | flops 10574853 | bytes 510433 | solution.py:111
  146.1 1.9 collective-permute-start.3
  148.4 4.5 collective-permute-start.2
  155.1 1.4 fusion.75
  158.6 316.7 %while.61 = (s32[]{:T(128)}, f32[12,64]{1,0:T(8,128)S(1)}, f32[64]{0:T(128)S(1)}, f32[64,64]{1,0:T(8,128)S(1)}, f32[64]{0:T(128)S(1)}, /*index=5*/f32[64,2]{0,1:...) while((s32[]{:T(128)}, f32[12,64]{1,0:T(8,128)S(1)}, ...), condition=%wide.region_6.7_spmd.clone, body=%wide.region_2.6_spmd.clone.sunk | while | flops 30749576 | bytes 3271488 | solution.py:131
  174.5 1.0 convert_reduce_fusion.16
  184.4 1.0 convert_reduce_fusion.16
  204.2 1.0 convert_reduce_fusion.16
  214.1 1.0 convert_reduce_fusion.16
  253.6 1.0 convert_reduce_fusion.16
  273.5 1.0 convert_reduce_fusion.16
  283.3 1.0 convert_reduce_fusion.16
  303.1 1.0 convert_reduce_fusion.16
  342.7 1.0 convert_reduce_fusion.16
  362.5 1.0 convert_reduce_fusion.16
  382.3 1.0 convert_reduce_fusion.16
  421.9 1.0 convert_reduce_fusion.16
  475.3 1.0 fusion.86
  476.5 2.1 fusion.84
  478.7 3.6 collective-permute-start.5
  482.3 1.3 collective-permute-start.4
  483.7 217.0 %while.60 = (s32[]{:T(128)}, f32[12,64]{1,0:T(8,128)S(1)}, f32[64]{0:T(128)S(1)}, f32[64,64]{1,0:T(8,128)S(1)}, f32[64]{0:T(128)S(1)}, /*index=5*/f32[64,2]{0,1:...) while((s32[]{:T(128)}, f32[12,64]{1,0:T(8,128)S(1)}, ...), condition=%wide.region_11.12_spmd, body=%wide.region_7.11_spmd.sunk | while | flops 30744452 | bytes 2218369 | solution.py:131
  700.7 42.2 %all-reduce = (f32[12,64]{1,0:T(8,128)S(1)}, f32[64]{0:T(128)S(1)}, f32[64,64]{1,0:T(8,128)S(1)}, f32[64]{0:T(128)S(1)}, f32[64,2]{0,1:T(2,128)S(1)}, /*index=5*/f32[2]{0:T(128)S(1)}) all-reduce(f32[12,64]{1,0:T(8,128)S(1)} %get-tuple-element.299, f32[64]{0:T(128)S(1)} %get-tuple-element.300, ...), channel_id=1, replica_groups=mesh['grp'=4,'col'=8] {'grp','col'}, use_global_device_ids=true, to_apply=%region_12.13 | all-reduce | flops 5122 | bytes 40976 | tf_op jit(solution)/shard_map/psum | solution.py:207
  746.0 1.9 collective-permute-start.6
  747.9 2.4 collective-permute-start.7
  750.8 2.6 collective-permute-done.6
  753.4 4.4 collective-permute-done.7
  (3013 shorter events, 467.6 us)
Async XLA Ops:
  6.3 148.6 %copy-start.2 = (f32[1,32,8,128]{3,2,1,0:T(8,128)}, f32[1,32,8,128]{3,2,1,0:T(8,128)S(1)}, u32[]{:S(2)}) copy-start(f32[1,32,8,128]{3,2,1,0:T(8,128)S(1)} %get-tuple-element.693) | copy-start | bytes 393220
  6.3 148.6 %copy-start.4 = (f32[32,8,128]{2,1,0:T(8,128)}, f32[32,8,128]{2,1,0:T(8,128)S(1)}, u32[]{:S(2)}) copy-start(f32[32,8,128]{2,1,0:T(8,128)S(1)} %get-tuple-element.752) | copy-start | bytes 393220
  10.2 133.7 %collective-permute-start = (f32[4,32,1,128]{3,2,1,0:T(1,128)S(1)}, f32[4,32,1,128]{3,2,1,0:T(1,128)S(1)}, u32[]{:S(2)}, u32[]{:S(2)}) collective-permute-start(f32[4,32,1,128]{3,2,1,0:T(1,128)S(1)} %get-tuple-element.725), channel_id=1, source_target_pairs={{8,0},{16,8},{24,16},{9,1},{17,9},{25,17},{10,2},{18,10},{26,18},{... | collective-permute-start | bytes 196616 | tf_op jit(solution)/shard_map/ppermute | solution.py:20
  11.5 132.4 %collective-permute-start.1 = (f32[4,32,1,128]{3,2,1,0:T(1,128)S(1)}, f32[4,32,1,128]{3,2,1,0:T(1,128)S(1)}, u32[]{:S(2)}, u32[]{:S(2)}) collective-permute-start(f32[4,32,1,128]{3,2,1,0:T(1,128)S(1)} %get-tuple-element.724), channel_id=1, source_target_pairs={{0,8},{8,16},{16,24},{1,9},{9,17},{17,25},{2,10},{10,18},{18,26},{... | collective-permute-start | bytes 196616 | tf_op jit(solution)/shard_map/ppermute | solution.py:17
  143.8 9.1 %copy-start.10 = (f32[32,8,128]{2,1,0:T(8,128)}, f32[32,8,128]{2,1,0:T(8,128)S(1)}, u32[]{:S(2)}) copy-start(f32[32,8,128]{2,1,0:T(8,128)S(1)} %get-tuple-element.690) | copy-start | bytes 393220
  146.1 7.6 collective-permute-start.3
  148.4 6.0 collective-permute-start.2
  478.6 5.0 copy-start.11
  478.7 267.1 %collective-permute-start.5 = (f32[2,32,1,128]{3,2,1,0:T(1,128)S(1)}, f32[2,32,1,128]{3,2,1,0:T(1,128)S(1)}, u32[]{:S(2)}, u32[]{:S(2)}) collective-permute-start(f32[2,32,1,128]{3,2,1,0:T(1,128)S(1)} %get-tuple-element.737), channel_id=1, source_target_pairs={{0,8},{8,16},{16,24},{1,9},{9,17},{17,25},{2,10},{10,18},{18,26},{... | collective-permute-start | bytes 98312 | tf_op jit(solution)/shard_map/ppermute | solution.py:17
  482.3 263.4 %collective-permute-start.4 = (f32[2,32,1,128]{3,2,1,0:T(1,128)S(1)}, f32[2,32,1,128]{3,2,1,0:T(1,128)S(1)}, u32[]{:S(2)}, u32[]{:S(2)}) collective-permute-start(f32[2,32,1,128]{3,2,1,0:T(1,128)S(1)} %get-tuple-element.736), channel_id=1, source_target_pairs={{8,0},{16,8},{24,16},{9,1},{17,9},{25,17},{10,2},{18,10},{26,18},{... | collective-permute-start | bytes 98312 | tf_op jit(solution)/shard_map/ppermute | solution.py:20
  483.7 4.0 copy-start.36
  490.5 4.0 copy-start.36
  510.8 4.0 copy-start.36
  517.6 4.0 copy-start.36
  551.5 4.0 copy-start.36
  565.0 4.0 copy-start.36
  578.6 4.0 copy-start.36
  585.4 4.0 copy-start.36
  592.1 4.0 copy-start.36
  598.9 4.0 copy-start.36
  605.7 4.0 copy-start.36
  612.5 4.0 copy-start.36
  619.3 4.0 copy-start.36
  632.9 4.0 copy-start.36
  653.2 4.0 copy-start.36
  666.7 4.0 copy-start.36
  680.3 4.0 copy-start.36
  687.1 4.0 copy-start.36
  693.9 4.0 copy-start.36
  746.0 7.5 collective-permute-start.6
  747.9 9.9 %collective-permute-start.7 = (f32[2,32,10,1]{3,1,2,0:T(8,128)S(1)}, f32[2,32,10,1]{3,1,2,0:T(8,128)S(1)}, u32[]{:S(2)}, u32[]{:S(2)}) collective-permute-start(f32[2,32,10,1]{3,1,2,0:T(8,128)S(1)} %get-tuple-element.733), channel_id=1, source_target_pairs={{0,1},{1,2},{2,3},{3,4},{4,5},{5,6},{6,7},{8,9},{9,10},{10,11},{11... | collective-permute-start | bytes 7688 | tf_op jit(solution)/shard_map/ppermute | solution.py:17
  750.8 7.3 copy-start.12
  (520 other events, 706.2 us)
where the time goes:
time: 773 us; the launch traced here: 759 us
  local copies, waits for them, and re-layouts  287 us (37%)
  loops' own time  196 us (25%)
  matrix products  150 us (19%)
  other arithmetic  55.1 us (7%)
  blocking collectives  42.2 us (5%)
  starting transfers between devices  21.5 us (3%)
    while x1600, local copies, waits for them, and re-layouts  176 us
    another operation x2, loops' own time, backward_lines(): lax.scan(backward_one_line, running, jnp.arange(solid.shape[0], dtype=jnp...  131 us
    another operation x1, loops' own time, forward_coupling(): lax.map(forward_one_line, jnp.arange(solid.shape[0], dtype=jnp.int32))  64.3 us
    dynamic_slice x96, local copies, waits for them, and re-layouts, forward_coupling(): lax.map(forward_one_line, jnp.arange(solid.shape[0], dtype=jnp.int32))  56 us
    psum x1, blocking collectives, shards(): lax.psum((running[0], running[1], running[2], running[3], running[4], run...  42.2 us
    dot_general x64, matrix products, backprop(): jnp.dot(w_out, d_logits, preferred_element_type=jnp.float32)  42 us
    dot_general x96, matrix products, network(): jnp.dot(w_mid.T, hidden_one, preferred_element_type=jnp.float32)  27.2 us
    dynamic_slice x64, local copies, waits for them, and re-layouts, backward_one_line(): d_line = lax.dynamic_index_in_dim(d_coupling, line_index, 0, keepdims=False)  22.2 us
  transfers between devices with their start and end apart: 8, of which 3 were waited for; matrix products, arithmetic and copies ran while one was open for 26% of the time, Pallas kernels for 0%

commit v1 on v0

v1 whole, which is shorter than its diff:
```python
import functools
import math

import jax
import jax.numpy as jnp
from jax import lax
from jax.experimental import pallas as pl
from jax.experimental.pallas import tpu as pltpu
from jax.sharding import PartitionSpec as P

time_step = 0.15
loss_gain = 16.0
MESH = pl.DeviceIdType.MESH
f32 = jnp.float32
bf16 = jnp.bfloat16
TILE = 16
LOG = 8


def gates(logit):
    small = jnp.exp(-jnp.abs(logit))
    soft = jnp.maximum(logit, 0.0) + jnp.log1p(small)
    sig = jnp.where(logit >= 0.0, 1.0, small) / (1.0 + small)
    return soft, sig


def kernel(
    ngrp, ncol, scale, zb,
    desc_ref, s_ref, f_ref, mat_ref, mask_ref, scond_ref, fcond_ref,
    w_in_ref, b_in_ref, w_mid_ref, b_mid_ref, w_out_t_ref, b_out_ref, gs_ref, gf_ref,
    adj_s_ref, adj_f_ref, g_w_in_ref, g_b_in_ref, g_w_mid_ref, g_b_mid_ref, g_w_out_ref, g_b_out_ref,
    aug_ref, fd_ref, h1_ref, h2_ref, lg0_ref, lg_ref, free_ref, us_ref, ps_ref, g2_ref,
    halo_ref, grad_ref, xs_ref, xr_ref, ys_ref, yr_ref, xs2_ref, xr2_ref, ys2_ref, yr2_ref,
    acc_ref, part_ref, grp_ref, fin_ref,
    hs_sem, hr_sem, hs2_sem, hr2_sem, c_ssem, c_rsem, g_ssem, g_rsem, a_ssem, a_rsem,
):
    ndesc, nz, nx, ny = desc_ref.shape
    hid = w_mid_ref.shape[0]
    rows = nz * nx
    cells = nx * ny
    row_s, row_one, row_d, row_two = ndesc, ndesc + 2, ndesc + 3, ndesc + 5
    me_g = lax.axis_index("grp")
    me_c = lax.axis_index("col")

    def grp_peer(k):
        return (lax.rem(me_g + (k + ngrp), ngrp), me_c)

    def col_peer(k):
        return (me_g, lax.rem(me_c + (k + ncol), ncol))

    barrier = pltpu.get_barrier_semaphore()
    for k in range(1, ngrp):
        pl.semaphore_signal(barrier, inc=1, device_id=grp_peer(k), device_id_type=MESH)
    for k in range(1, ncol):
        pl.semaphore_signal(barrier, inc=1, device_id=col_peer(k), device_id_type=MESH)

    def remote(src, dst, ssem, rsem, peer):
        return pltpu.make_async_remote_copy(
            src_ref=src, dst_ref=dst, send_sem=ssem, recv_sem=rsem, device_id=peer, device_id_type=MESH
        )

    xi = lax.broadcasted_iota(jnp.int32, (nx, ny), 0)
    yi = lax.broadcasted_iota(jnp.int32, (nx, ny), 1)

    mat = mat_ref[...]
    free = time_step * (1.0 - mask_ref[...].astype(f32))
    free_ref[...] = free
    sk = jnp.zeros((rows, ny), f32)
    fk = jnp.zeros((rows, ny), f32)
    for kind in range(scond_ref.shape[0]):
        sk = sk + jnp.where(mat == kind, scond_ref[kind], 0.0)
        fk = fk + jnp.where(mat == kind, fcond_ref[kind], 0.0)
    us_ref[0:rows, :] = sk * free
    us_ref[rows : 2 * rows, :] = fk * free
    ps_ref[0:rows, :] = us_ref[0:rows, :] * gs_ref[...]
    ps_ref[rows : 2 * rows, :] = us_ref[rows : 2 * rows, :] * gf_ref[...]

    def stage_edges(refs, xsend, ysend):
        for i, (ref, base) in enumerate(refs):
            xsend[0, i] = ref[pl.ds(base, nz, stride=nx), :]
            xsend[1, i] = ref[pl.ds(base + nx - 1, nz, stride=nx), :]
            turned = jnp.transpose(ref[base : base + rows, :])
            ysend[0, i : i + 1, :] = turned[0:1, :]
            ysend[1, i : i + 1, :] = turned[ny - 1 : ny, :]

    def halo_copies(xsend, xrecv, ysend, yrecv, ssem, rsem):
        return [
            remote(xsend.at[0], xrecv.at[0], ssem.at[0], rsem.at[0], grp_peer(-1)),
            remote(xsend.at[1], xrecv.at[1], ssem.at[1], rsem.at[1], grp_peer(1)),
            remote(ysend.at[0], yrecv.at[0], ssem.at[2], rsem.at[2], col_peer(-1)),
            remote(ysend.at[1], yrecv.at[1], ssem.at[3], rsem.at[3], col_peer(1)),
        ]

    not_first_g = jnp.where(me_g == 0, 0.0, 1.0).astype(f32)
    not_last_g = jnp.where(me_g == ngrp - 1, 0.0, 1.0).astype(f32)
    not_first_c = jnp.where(me_c == 0, 0.0, 1.0).astype(f32)
    not_last_c = jnp.where(me_c == ncol - 1, 0.0, 1.0).astype(f32)

    def place_halo(count, xrecv, yrecv):
        line = lax.broadcasted_iota(jnp.int32, (ny, rows), 0)
        for i in range(count):
            low = yrecv[1, i : i + 1, :] * not_first_c
            high = yrecv[0, i : i + 1, :] * not_last_c
            edge = jnp.where(line == 0, low, 0.0) + jnp.where(line == ny - 1, high, 0.0)
            base = i * rows
            halo_ref[base : base + rows, :] = jnp.transpose(edge)
            at_low = pl.ds(base, nz, stride=nx)
            at_high = pl.ds(base + nx - 1, nz, stride=nx)
            halo_ref[at_low, :] = halo_ref[at_low, :] + xrecv[1, i] * not_first_g
            halo_ref[at_high, :] = halo_ref[at_high, :] + xrecv[0, i] * not_last_g

    def lap(v, halo):
        up = jnp.where(xi > 0, pltpu.roll(v, 1, 0), 0.0)
        down = jnp.where(xi < nx - 1, pltpu.roll(v, nx - 1, 0), 0.0)
        left = jnp.where(yi > 0, pltpu.roll(v, 1, 1), 0.0)
        right = jnp.where(yi < ny - 1, pltpu.roll(v, ny - 1, 1), 0.0)
        return (up + down) + (left + right) + halo - 4.0 * v

    stage_edges([(s_ref, 0), (f_ref, 0), (ps_ref, 0), (ps_ref, rows)], xs_ref, ys_ref)
    pl.semaphore_wait(barrier, ngrp + ncol - 2)
    first = halo_copies(xs_ref, xr_ref, ys_ref, yr_ref, hs_sem, hr_sem)
    for copy in first:
        copy.start()

    wide = aug_ref.shape[1]

    def split(b):
        high = b.astype(bf16).astype(f32)
        return high, b - high

    def turned_weights(pieces):
        aug_ref[...] = jnp.zeros(aug_ref.shape, f32)
        for at, value in pieces:
            aug_ref[at : at + value.shape[0], 0:hid] = value
        return jnp.transpose(aug_ref[...])

    b1_high, b1_low = split(b_in_ref[...])
    b2_high, b2_low = split(b_mid_ref[...])
    w_in = w_in_ref[...].astype(f32)
    w_out_t = w_out_t_ref[...].astype(f32)
    turned = turned_weights([(0, w_in), (row_one, b1_high), (row_two, b1_low), (TILE + row_d, w_out_t)])
    w1 = turned[0:hid, 0:TILE].astype(bf16)
    wo = turned[0:hid, TILE : 2 * TILE].astype(bf16)
    turned = turned_weights([(0, w_mid_ref[...].astype(f32)), (hid + row_one, b2_high), (hid + row_two, b2_low)])
    w2 = turned[0:hid, 0 : hid + TILE].astype(bf16)
    wm = w_mid_ref[...]
    aug_ref[...] = jnp.zeros(aug_ref.shape, f32)
    aug_ref[0:2, 0:hid] = w_out_t
    aug_ref[LOG : LOG + 2, 0:hid] = w_in[ndesc : ndesc + 2, :]
    w3 = aug_ref[0:LOG, 0:hid].astype(bf16)
    wd = aug_ref[LOG : 2 * LOG, 0:hid].astype(bf16)
    b_out_0 = b_out_ref[0, 0]
    b_out_1 = b_out_ref[0, 1]

    grad_ref[...] = jnp.zeros(grad_ref.shape, f32)

    def dot(a, b):
        return jnp.dot(a, b, preferred_element_type=f32)

    def set_row(z, row, value):
        fd_ref[pl.ds(pl.multiple_of(z * (nx * TILE), nx * TILE) + row, nx, stride=TILE), :] = value

    def tile(z):
        base = pl.multiple_of(z * (nx * TILE), nx * TILE)
        block = fd_ref[pl.ds(base, nx * TILE), :].astype(bf16)
        return jnp.concatenate([block[x * TILE : (x + 1) * TILE, :] for x in range(nx)], axis=1)

    def put_log(ref, z, value):
        for x in range(nx):
            at = pl.multiple_of(z * (nx * LOG), nx * LOG) + x * LOG
            ref[pl.ds(at, LOG), :] = value[:, x * ny : (x + 1) * ny]

    def get_log(ref, z, row):
        return ref[pl.ds(pl.multiple_of(z * (nx * LOG), nx * LOG) + row, nx, stride=LOG), :]

    def field(ref, z, which=0):
        return ref[pl.ds(pl.multiple_of(z * nx, nx) + which * rows, nx), :]

    def put_field(ref, z, value, which=0):
        ref[pl.ds(pl.multiple_of(z * nx, nx) + which * rows, nx), :] = value

    def layers(fds):
        h1 = [jnp.tanh(dot(w1, fd)).astype(bf16) for fd in fds]
        h2 = [jnp.tanh(dot(w2, jnp.concatenate([h, fd], axis=0))).astype(bf16) for h, fd in zip(h1, fds)]
        logits = [dot(w3, h) for h in h2]
        return h1, h2, logits

    def through(d, h):
        wide_h = h.astype(f32)
        return (d * (1.0 - wide_h * wide_h)).astype(bf16)

    def layers_back(fds, h1, h2, zs):
        d2 = [through(dot(wo, fd), h) for fd, h in zip(fds, h2)]
        d1 = [through(dot(wm, d), h) for d, h in zip(d2, h1)]
        for z, d in zip(zs, d1):
            put_log(lg_ref, z, dot(wd, d))
        total = grad_ref[:, 0 : 3 * hid + TILE]
        for i in range(len(zs)):
            left = jnp.concatenate([fds[i], h1[i]], axis=0)
            right = jnp.concatenate([d1[i], d2[i], h2[i], fds[i]], axis=0)
            total = total + lax.dot_general(
                left, right, (((1,), (1,)), ((), ())), preferred_element_type=f32
            )
        grad_ref[:, 0 : 3 * hid + TILE] = total

    ones = jnp.ones((nx, ny), f32)
    nil = jnp.zeros((nx, ny), f32)

    def start_body(step, _):
        zs = [step * zb + i for i in range(zb)]
        for z in zs:
            for d in range(ndesc):
                set_row(z, d, desc_ref[d, z].astype(f32))
            set_row(z, row_s, field(s_ref, z))
            set_row(z, row_s + 1, field(f_ref, z))
            set_row(z, row_one, ones)
            set_row(z, row_d, nil)
            set_row(z, row_d + 1, nil)
            set_row(z, row_two, ones)
        fds = [tile(z) for z in zs]
        h1, h2, logits = layers(fds)
        for z, a, b, c in zip(zs, h1, h2, logits):
            h1_ref[z] = a
            h2_ref[z] = b
            put_log(lg0_ref, z, c)
        return 0

    lax.fori_loop(0, nz // zb, start_body, 0)

    for copy in first:
        copy.wait()
    place_halo(4, xr_ref, yr_ref)

    def logit_cots(z, dcoup, ref):
        h_sf, h_sig = gates(get_log(ref, z, 0) + b_out_0)
        a_sf, a_sig = gates(get_log(ref, z, 1) + b_out_1)
        set_row(z, row_d, dcoup * a_sf * h_sig)
        set_row(z, row_d + 1, dcoup * h_sf * a_sig)
        return h_sf * a_sf

    def later_body(step, _):
        zs = [step * zb + i for i in range(zb)]
        diff = []
        for z in zs:
            h_sf = gates(get_log(lg0_ref, z, 0) + b_out_0)[0]
            a_sf = gates(get_log(lg0_ref, z, 1) + b_out_1)[0]
            solid, fluid, free = field(s_ref, z), field(f_ref, z), field(free_ref, z)
            swap = free * (h_sf * a_sf) * (fluid - solid)
            solid_1 = solid + field(us_ref, z) * lap(solid, field(halo_ref, z)) + swap
            fluid_1 = fluid + field(us_ref, z, 1) * lap(fluid, field(halo_ref, z, 1)) - swap
            set_row(z, row_s, solid_1)
            set_row(z, row_s + 1, fluid_1)
            diff.append(fluid_1 - solid_1)
        fds = [tile(z) for z in zs]
        h1, h2, logits = layers(fds)
        for z, c in zip(zs, logits):
            put_log(lg_ref, z, c)
        swing = []
        for z, d in zip(zs, diff):
            turn = field(free_ref, z) * (field(gs_ref, z) - field(gf_ref, z))
            swing.append(logit_cots(z, d * turn, lg_ref) * turn)
        fds = [tile(z) for z in zs]
        layers_back(fds, h1, h2, zs)
        for z, w in zip(zs, swing):
            new_s = field(gs_ref, z) + lap(field(ps_ref, z), field(halo_ref, z, 2)) - w + get_log(lg_ref, z, 0)
            new_f = field(gf_ref, z) + lap(field(ps_ref, z, 1), field(halo_ref, z, 3)) + w + get_log(lg_ref, z, 1)
            put_field(g2_ref, z, new_s)
            put_field(g2_ref, z, new_f, 1)
            put_field(ps_ref, z, field(us_ref, z) * new_s)
            put_field(ps_ref, z, field(us_ref, z, 1) * new_f, 1)
        return 0

    lax.fori_loop(0, nz // zb, later_body, 0)

    stage_edges([(ps_ref, 0), (ps_ref, rows)], xs2_ref, ys2_ref)
    second = halo_copies(xs2_ref, xr2_ref, ys2_ref, yr2_ref, hs2_sem, hr2_sem)
    for copy in second:
        copy.start()

    def first_body(step, _):
        zs = [step * zb + i for i in range(zb)]
        swing = []
        for z in zs:
            solid, fluid = field(s_ref, z), field(f_ref, z)
            set_row(z, row_s, solid)
            set_row(z, row_s + 1, fluid)
            turn = field(free_ref, z) * (field(g2_ref, z) - field(g2_ref, z, 1))
            swing.append(logit_cots(z, (fluid - solid) * turn, lg0_ref) * turn)
        fds = [tile(z) for z in zs]
        layers_back(fds, [h1_ref[z] for z in zs], [h2_ref[z] for z in zs], zs)
        for z, w in zip(zs, swing):
            put_field(g2_ref, z, field(g2_ref, z) - w + get_log(lg_ref, z, 0))
            put_field(g2_ref, z, field(g2_ref, z, 1) + w + get_log(lg_ref, z, 1), 1)
        return 0

    lax.fori_loop(0, nz // zb, first_body, 0)

    piece = acc_ref.shape[1]
    lane = lax.broadcasted_iota(jnp.int32, (hid // 2, 2 * hid), 1)
    half = hid // 2
    wide_l = 2 * hid
    packed = jnp.concatenate(
        [
            grad_ref[0:TILE, 0:wide_l],
            jnp.where(
                lane >= hid,
                grad_ref[TILE : TILE + half, 0:wide_l],
                pltpu.roll(grad_ref[TILE + half : TILE + hid, 0:wide_l], hid, 1),
            ),
            grad_ref[TILE - LOG : TILE, wide_l : 2 * wide_l],
            jnp.zeros((ncol * piece - TILE - half - LOG, wide_l), f32),
        ],
        axis=0,
    )
    for i in range(ncol):
        acc_ref[i] = packed[i * piece : (i + 1) * piece, :]
    sends = []
    for k in range(1, ncol):
        dev = col_peer(k)
        sends.append(remote(acc_ref.at[dev[1]], part_ref.at[k - 1], c_ssem.at[k - 1], c_rsem.at[k - 1], dev))
    for copy in sends:
        copy.start()

    for copy in second:
        copy.wait()
    place_halo(2, xr2_ref, yr2_ref)

    for copy in sends:
        copy.wait()
    own = acc_ref[me_c]
    for k in range(ncol - 1):
        own = own + part_ref[k]
    grp_ref[me_g] = own
    sends = []
    for k in range(1, ngrp):
        sends.append(
            remote(grp_ref.at[me_g], grp_ref.at[me_g], g_ssem.at[k - 1], g_rsem.at[k - 1], grp_peer(k))
        )
    for copy in sends:
        copy.start()

    def final_body(z, _):
        adj_s_ref[pl.ds(pl.multiple_of(z * nx, nx), nx), :] = field(g2_ref, z) + lap(
            field(ps_ref, z), field(halo_ref, z)
        )
        adj_f_ref[pl.ds(pl.multiple_of(z * nx, nx), nx), :] = field(g2_ref, z, 1) + lap(
            field(ps_ref, z, 1), field(halo_ref, z, 1)
        )
        return 0

    lax.fori_loop(0, nz, final_body, 0, unroll=zb)

    for copy in sends:
        copy.wait()
    own = grp_ref[0]
    for k in range(1, ngrp):
        own = own + grp_ref[k]
    fin_ref[me_c] = own * scale
    sends = []
    for k in range(1, ncol):
        sends.append(remote(fin_ref.at[me_c], fin_ref.at[me_c], a_ssem.at[k - 1], a_rsem.at[k - 1], col_peer(k)))
    for copy in sends:
        copy.start()
    for copy in sends:
        copy.wait()
    whole = jnp.concatenate([fin_ref[i] for i in range(ncol)], axis=0)
    g_w_in_ref[...] = whole[0 : ndesc + 2, 0:hid]
    ones_row = whole[row_one : row_one + 1, :]
    g_b_in_ref[...] = ones_row[:, 0:hid]
    g_b_mid_ref[...] = pltpu.roll(ones_row, hid, 1)[:, 0:hid]
    mid = whole[TILE : TILE + half, :]
    g_w_mid_ref[0:half, :] = pltpu.roll(mid, hid, 1)[:, 0:hid]
    g_w_mid_ref[half:hid, :] = mid[:, 0:hid]
    at = TILE + half + row_d - (TILE - LOG)
    g_w_out_ref[...] = whole[at : at + 2, 0:hid]
    one_lane = hid + row_one
    b0 = pltpu.roll(whole[at : at + 1, :], wide_l - one_lane, 1)
    b1 = pltpu.roll(whole[at + 1 : at + 2, :], wide_l - one_lane + 1, 1)
    first_lane = lax.broadcasted_iota(jnp.int32, (1, wide_l), 1) == 0
    g_b_out_ref[...] = jnp.where(first_lane, b0, b1)[:, 0:2]


def solution(mesh):
    ngrp, ncol = mesh.shape["grp"], mesh.shape["col"]

    def shards(
        descriptors, solid_temp, fluid_temp, material, fixed_mask, solid_cond, fluid_cond,
        w_in, b_in, w_mid, b_mid, w_out, b_out, solid_cot, fluid_cot,
    ):
        ndesc, nz, nx, ny = descriptors.shape
        feat, hid = w_in.shape
        rows = nz * nx
        zb = next(k for k in (4, 2, 1) if nz % k == 0)
        scale = loss_gain / math.sqrt(rows * ny * ngrp * ncol)
        used = TILE + hid // 2 + LOG
        piece = 8 * -(-used // (8 * ncol))
        flat = lambda a: a.reshape(rows, ny)
        vmem = pl.BlockSpec(memory_space=pltpu.VMEM)
        smem = pl.BlockSpec(memory_space=pltpu.SMEM)
        sds = jax.ShapeDtypeStruct
        outs = pl.pallas_call(
            functools.partial(kernel, ngrp, ncol, scale, zb),
            out_shape=(
                sds((rows, ny), f32), sds((rows, ny), f32), sds((feat, hid), f32), sds((1, hid), f32),
                sds((hid, hid), f32), sds((1, hid), f32), sds((2, hid), f32), sds((1, 2), f32),
            ),
            in_specs=[vmem] * 5 + [smem] * 2 + [vmem] * 5 + [smem] + [vmem] * 2,
            out_specs=(vmem,) * 8,
            scratch_shapes=[
                pltpu.VMEM((128, 128), f32),
                pltpu.VMEM((rows * TILE, ny), f32),
                pltpu.VMEM((nz, hid, nx * ny), bf16),
                pltpu.VMEM((nz, hid, nx * ny), bf16),
                pltpu.VMEM((rows * LOG, ny), f32),
                pltpu.VMEM((rows * LOG, ny), f32),
                pltpu.VMEM((rows, ny), f32),
                pltpu.VMEM((2 * rows, ny), f32),
                pltpu.VMEM((2 * rows, ny), f32),
                pltpu.VMEM((2 * rows, ny), f32),
                pltpu.VMEM((4 * rows, ny), f32),
                pltpu.VMEM((TILE + hid, 4 * hid), f32),
                pltpu.VMEM((2, 4, nz, ny), f32),
                pltpu.VMEM((2, 4, nz, ny), f32),
                pltpu.VMEM((2, 4, rows), f32),
                pltpu.VMEM((2, 4, rows), f32),
                pltpu.VMEM((2, 2, nz, ny), f32),
                pltpu.VMEM((2, 2, nz, ny), f32),
                pltpu.VMEM((2, 2, rows), f32),
                pltpu.VMEM((2, 2, rows), f32),
                pltpu.VMEM((ncol, piece, 2 * hid), f32),
                pltpu.VMEM((ncol - 1, piece, 2 * hid), f32),
                pltpu.VMEM((ngrp, piece, 2 * hid), f32),
                pltpu.VMEM((ncol, piece, 2 * hid), f32),
                pltpu.SemaphoreType.DMA((4,)),
                pltpu.SemaphoreType.DMA((4,)),
                pltpu.SemaphoreType.DMA((4,)),
                pltpu.SemaphoreType.DMA((4,)),
                pltpu.SemaphoreType.DMA((ncol - 1,)),
                pltpu.SemaphoreType.DMA((ncol - 1,)),
                pltpu.SemaphoreType.DMA((ngrp - 1,)),
                pltpu.SemaphoreType.DMA((ngrp - 1,)),
                pltpu.SemaphoreType.DMA((ncol - 1,)),
                pltpu.SemaphoreType.DMA((ncol - 1,)),
            ],
            compiler_params=pltpu.CompilerParams(
                collective_id=0, has_side_effects=True, vmem_limit_bytes=48 * 1024 * 1024
            ),
            name="wick_adjoint",
        )(
            descriptors, flat(solid_temp), flat(fluid_temp), flat(material), flat(fixed_mask),
            solid_cond, fluid_cond, w_in, b_in.reshape(1, hid), w_mid, b_mid.reshape(1, hid),
            w_out.T, b_out.reshape(1, 2), flat(solid_cot), flat(fluid_cot),
        )
        block = lambda a: a.reshape(nz, nx, ny)
        return (
            block(outs[0]), block(outs[1]), outs[2], outs[3].reshape(hid),
            outs[4], outs[5].reshape(hid), outs[6].T, outs[7].reshape(2),
        )

    plane = P(None, "grp", "col")
    return jax.shard_map(
        shards,
        mesh=mesh,
        in_specs=(P(None, None, "grp", "col"),) + (plane,) * 4 + (P(),) * 8 + (plane,) * 2,
        out_specs=(plane, plane) + (P(),) * 6,
        check_vma=False,
    )
```

time: 773 us -> 58.6 us (0.08)
  the two profiles are of different devices: /device:TPU:4 before, /device:TPU:0 now
where the time goes in v1:
time: 58.6 us; the launch traced here: 58.3 us
  Pallas kernels  44.4 us (76%)
  local copies, waits for them, and re-layouts  13.1 us (22%)
  between operations  0.73 us (1%)
    pallas_call x1, Pallas kernels, shards(): pl.pallas_call(functools.partial(kernel, ngrp, ncol, scale, zb), out_shap...  44.4 us
    unnamed x38, local copies, waits for them, and re-layouts  13.1 us

profile of v1, /device:TPU:0, one launch (start us, length us, event | category | flops | bytes accessed | tf_op | source)
XLA Modules:
  0.0 58.3 jit_solution(14671091173533802166)
XLA Ops:
  0.6 0.0 copy-start.7
  0.6 0.0 copy-start.12
  0.7 0.0 copy-start.13
  0.7 0.0 copy-start.9
  0.7 0.0 copy-start.10
  0.7 0.0 copy-start.11
  0.7 0.7 %copy-done.7 = bf16[64,64]{1,0:T(8,128)(2,1)S(1)} copy-done((bf16[64,64]{1,0:T(8,128)(2,1)S(1)}, bf16[64,64]{1,0:T(8,128)(2,1)}, u32[]{:S(2)}) %copy-start.7) | copy-done | bytes 8216
  1.4 0.0 copy-done.12
  1.4 0.0 copy-done.13
  1.4 0.0 copy-done.9
  1.4 0.0 copy-done.10
  1.4 0.0 copy-done.11
  1.4 0.0 copy-start
  1.4 1.1 %copy-done = bf16[10,32,8,128]{3,2,1,0:T(8,128)(2,1)S(1)} copy-done((bf16[10,32,8,128]{3,2,1,0:T(8,128)(2,1)S(1)}, bf16[10,32,8,128]{3,2,1,0:T(8,128)(2,1)}, u32[]{:S(2)}) %copy-start) | copy-done | bytes 655384
  2.5 0.0 copy-start.1
  2.5 0.9 %copy-done.1 = f32[32,8,128]{2,1,0:T(8,128)S(1)} copy-done((f32[32,8,128]{2,1,0:T(8,128)S(1)}, f32[32,8,128]{2,1,0:T(8,128)}, u32[]{:S(2)}) %copy-start.1) | copy-done | bytes 131096
  3.4 0.9 %copy-done.2 = f32[32,8,128]{2,1,0:T(8,128)S(1)} copy-done((f32[32,8,128]{2,1,0:T(8,128)S(1)}, f32[32,8,128]{2,1,0:T(8,128)}, u32[]{:S(2)}) %copy-start.2) | copy-done | bytes 131096
  4.3 0.9 %copy-done.3 = s32[32,8,128]{2,1,0:T(8,128)S(1)} copy-done((s32[32,8,128]{2,1,0:T(8,128)S(1)}, s32[32,8,128]{2,1,0:T(8,128)}, u32[]{:S(2)}) %copy-start.3) | copy-done | bytes 131096
  5.2 0.9 %copy-done.4 = s32[32,8,128]{2,1,0:T(8,128)S(1)} copy-done((s32[32,8,128]{2,1,0:T(8,128)S(1)}, s32[32,8,128]{2,1,0:T(8,128)}, u32[]{:S(2)}) %copy-start.4) | copy-done | bytes 131096
  6.1 0.9 %copy-done.5 = f32[32,8,128]{2,1,0:T(8,128)S(1)} copy-done((f32[32,8,128]{2,1,0:T(8,128)S(1)}, f32[32,8,128]{2,1,0:T(8,128)}, u32[]{:S(2)}) %copy-start.5) | copy-done | bytes 131096
  7.0 0.9 %copy-done.6 = f32[32,8,128]{2,1,0:T(8,128)S(1)} copy-done((f32[32,8,128]{2,1,0:T(8,128)S(1)}, f32[32,8,128]{2,1,0:T(8,128)}, u32[]{:S(2)}) %copy-start.6) | copy-done | bytes 131096
  7.9 0.7 %copy-done.8 = bf16[12,64]{1,0:T(8,128)(2,1)S(1)} copy-done((bf16[12,64]{1,0:T(8,128)(2,1)S(1)}, bf16[12,64]{1,0:T(8,128)(2,1)}, u32[]{:S(2)}) %copy-start.8) | copy-done | bytes 1560
  8.6 0.7 %copy-done.14 = f32[2]{0:T(128)S(1)} copy-done((f32[2]{0:T(128)S(1)}, f32[2]{0:T(128)}, u32[]{:S(2)}) %copy-start.14) | copy-done | bytes 32
  9.2 44.4 %wick_adjoint.1 = (f32[256,128]{1,0:T(8,128)S(1)}, f32[256,128]{1,0:T(8,128)S(1)}, f32[12,64]{1,0:T(8,128)S(1)}, f32[1,64]{1,0:T(1,128)S(1)}, f32[64,64]{1,0:T(8...) custom-call(bf16[10,32,8,128]{3,2,1,0:T(8,128)(2,1)S(1)} %copy-done, ...), custom_call_target="tpu_custom_call" | custom-call | tf_op jit(solution)/shard_map/wick_adjoint/pallas_call | solution.py:401
  53.6 0.7 %copy.31 = f32[32,8,128]{2,1,0:T(8,128)} copy(f32[32,8,128]{2,1,0:T(8,128)S(1)} %bitcast.23) | data formatting | bytes 262144
  54.3 0.7 %copy.32 = f32[32,8,128]{2,1,0:T(8,128)} copy(f32[32,8,128]{2,1,0:T(8,128)S(1)} %bitcast.22) | data formatting | bytes 262144
  55.0 0.6 %copy.33 = f32[12,64]{1,0:T(8,128)} copy(f32[12,64]{1,0:T(8,128)S(1)} %get-tuple-element.34) | data formatting | bytes 6144
  55.5 0.5 copy.34
  56.1 0.6 %copy.35 = f32[64,64]{1,0:T(8,128)} copy(f32[64,64]{1,0:T(8,128)S(1)} %get-tuple-element.36) | data formatting | bytes 32768
  56.7 0.5 copy.36
  57.2 0.6 copy.37
  57.7 0.5 copy.38
  (7 shorter events, 0.0 us)
Async XLA Ops:
  0.6 0.7 %copy-start.7 = (bf16[64,64]{1,0:T(8,128)(2,1)S(1)}, bf16[64,64]{1,0:T(8,128)(2,1)}, u32[]{:S(2)}) copy-start(bf16[64,64]{1,0:T(8,128)(2,1)} %w_mid_ref.1) | copy-start | bytes 24580
  0.6 0.7 %copy-start.12 = (f32[64]{0:T(128)S(1)}, f32[64]{0:T(128)}, u32[]{:S(2)}) copy-start(f32[64]{0:T(128)} %param.25) | copy-start | bytes 772
  0.7 0.7 %copy-start.13 = (bf16[64,2]{0,1:T(2,128)(2,1)S(1)}, bf16[64,2]{0,1:T(2,128)(2,1)}, u32[]{:S(2)}) copy-start(bf16[64,2]{0,1:T(2,128)(2,1)} %param.26) | copy-start | bytes 772
  0.7 0.7 %copy-start.9 = (f32[4]{0:T(128)S(1)}, f32[4]{0:T(128)}, u32[]{:S(2)}) copy-start(f32[4]{0:T(128)} %scond_ref.1) | copy-start | bytes 52
  0.7 0.7 %copy-start.10 = (f32[4]{0:T(128)S(1)}, f32[4]{0:T(128)}, u32[]{:S(2)}) copy-start(f32[4]{0:T(128)} %fcond_ref.1) | copy-start | bytes 52
  0.7 0.7 %copy-start.11 = (f32[64]{0:T(128)S(1)}, f32[64]{0:T(128)}, u32[]{:S(2)}) copy-start(f32[64]{0:T(128)} %param.23) | copy-start | bytes 772
  1.4 1.1 %copy-start = (bf16[10,32,8,128]{3,2,1,0:T(8,128)(2,1)S(1)}, bf16[10,32,8,128]{3,2,1,0:T(8,128)(2,1)}, u32[]{:S(2)}) copy-start(bf16[10,32,8,128]{3,2,1,0:T(8,128)(2,1)} %desc_ref.1) | copy-start | bytes 1966084
  2.5 0.9 %copy-start.1 = (f32[32,8,128]{2,1,0:T(8,128)S(1)}, f32[32,8,128]{2,1,0:T(8,128)}, u32[]{:S(2)}) copy-start(f32[32,8,128]{2,1,0:T(8,128)} %param.16) | copy-start | bytes 393220
  3.4 0.9 %copy-start.2 = (f32[32,8,128]{2,1,0:T(8,128)S(1)}, f32[32,8,128]{2,1,0:T(8,128)}, u32[]{:S(2)}) copy-start(f32[32,8,128]{2,1,0:T(8,128)} %param.17) | copy-start | bytes 393220
  4.3 0.9 %copy-start.3 = (s32[32,8,128]{2,1,0:T(8,128)S(1)}, s32[32,8,128]{2,1,0:T(8,128)}, u32[]{:S(2)}) copy-start(s32[32,8,128]{2,1,0:T(8,128)} %param.18) | copy-start | bytes 393220
  5.2 0.9 %copy-start.4 = (s32[32,8,128]{2,1,0:T(8,128)S(1)}, s32[32,8,128]{2,1,0:T(8,128)}, u32[]{:S(2)}) copy-start(s32[32,8,128]{2,1,0:T(8,128)} %param.19) | copy-start | bytes 393220
  6.1 0.9 %copy-start.5 = (f32[32,8,128]{2,1,0:T(8,128)S(1)}, f32[32,8,128]{2,1,0:T(8,128)}, u32[]{:S(2)}) copy-start(f32[32,8,128]{2,1,0:T(8,128)} %param.28) | copy-start | bytes 393220
  7.0 0.9 %copy-start.6 = (f32[32,8,128]{2,1,0:T(8,128)S(1)}, f32[32,8,128]{2,1,0:T(8,128)}, u32[]{:S(2)}) copy-start(f32[32,8,128]{2,1,0:T(8,128)} %param.29) | copy-start | bytes 393220
  7.9 0.7 %copy-start.8 = (bf16[12,64]{1,0:T(8,128)(2,1)S(1)}, bf16[12,64]{1,0:T(8,128)(2,1)}, u32[]{:S(2)}) copy-start(bf16[12,64]{1,0:T(8,128)(2,1)} %w_in_ref.1) | copy-start | bytes 4612
  8.6 0.7 %copy-start.14 = (f32[2]{0:T(128)S(1)}, f32[2]{0:T(128)}, u32[]{:S(2)}) copy-start(f32[2]{0:T(128)} %param.27) | copy-start | bytes 28

commit v2 on v1

--- a/solution.py
+++ b/solution.py
@@ -15,6 +15,7 @@
 bf16 = jnp.bfloat16
 TILE = 16
 LOG = 8
+FETCHED = 13
 
 
 def gates(logit):
@@ -26,18 +27,35 @@
 
 def kernel(
     ngrp, ncol, scale, zb,
-    desc_ref, s_ref, f_ref, mat_ref, mask_ref, scond_ref, fcond_ref,
-    w_in_ref, b_in_ref, w_mid_ref, b_mid_ref, w_out_t_ref, b_out_ref, gs_ref, gf_ref,
-    adj_s_ref, adj_f_ref, g_w_in_ref, g_b_in_ref, g_w_mid_ref, g_b_mid_ref, g_w_out_ref, g_b_out_ref,
+    w_in_ref, w_out_t_ref, *refs,
+):
+    sources, rest = refs[:FETCHED], refs[FETCHED:]
+    (
+    out_s_ref, out_f_ref, whole_ref, adj_s_ref, adj_f_ref, out_sem,
+    mask_ref, mat_ref, scond_ref, fcond_ref, gs_ref, gf_ref, s_ref, f_ref,
+    b_in_ref, b_mid_ref, w_mid_ref, b_out_ref, desc_ref, in_sem,
     aug_ref, fd_ref, h1_ref, h2_ref, lg0_ref, lg_ref, free_ref, us_ref, ps_ref, g2_ref,
     halo_ref, grad_ref, xs_ref, xr_ref, ys_ref, yr_ref, xs2_ref, xr2_ref, ys2_ref, yr2_ref,
     acc_ref, part_ref, grp_ref, fin_ref,
     hs_sem, hr_sem, hs2_sem, hr2_sem, c_ssem, c_rsem, g_ssem, g_rsem, a_ssem, a_rsem,
-):
-    ndesc, nz, nx, ny = desc_ref.shape
+    ) = rest
+    held = (
+        mask_ref, mat_ref, scond_ref, fcond_ref, gs_ref, gf_ref, s_ref, f_ref,
+        b_in_ref, b_mid_ref, w_mid_ref, b_out_ref, desc_ref,
+    )
+    fetches = [
+        pltpu.make_async_copy(source, place, in_sem.at[i])
+        for i, (source, place) in enumerate(zip(sources, held))
+    ]
+    for fetch in fetches:
+        fetch.start()
+    ndesc, _, ny = desc_ref.shape
+    nz = xs_ref.shape[2]
+    nx = s_ref.shape[0] // nz
     hid = w_mid_ref.shape[0]
     rows = nz * nx
-    cells = nx * ny
+    xw = max(1, 2 * 128 // ny)
+    xw = xw if nx % xw == 0 else 1
     row_s, row_one, row_d, row_two = ndesc, ndesc + 2, ndesc + 3, ndesc + 5
     me_g = lax.axis_index("grp")
     me_c = lax.axis_index("col")
@@ -62,14 +80,16 @@
     xi = lax.broadcasted_iota(jnp.int32, (nx, ny), 0)
     yi = lax.broadcasted_iota(jnp.int32, (nx, ny), 1)
 
+    for fetch in fetches[:8]:
+        fetch.wait()
     mat = mat_ref[...]
     free = time_step * (1.0 - mask_ref[...].astype(f32))
     free_ref[...] = free
     sk = jnp.zeros((rows, ny), f32)
     fk = jnp.zeros((rows, ny), f32)
-    for kind in range(scond_ref.shape[0]):
-        sk = sk + jnp.where(mat == kind, scond_ref[kind], 0.0)
-        fk = fk + jnp.where(mat == kind, fcond_ref[kind], 0.0)
+    for kind in range(scond_ref.shape[1]):
+        sk = sk + jnp.where(mat == kind, scond_ref[0:1, kind : kind + 1], 0.0)
+        fk = fk + jnp.where(mat == kind, fcond_ref[0:1, kind : kind + 1], 0.0)
     us_ref[0:rows, :] = sk * free
     us_ref[rows : 2 * rows, :] = fk * free
     ps_ref[0:rows, :] = us_ref[0:rows, :] * gs_ref[...]
@@ -122,6 +142,8 @@
     for copy in first:
         copy.start()
 
+    for fetch in fetches[8:]:
+        fetch.wait()
     wide = aug_ref.shape[1]
 
     def split(b):
@@ -149,8 +171,8 @@
     aug_ref[LOG : LOG + 2, 0:hid] = w_in[ndesc : ndesc + 2, :]
     w3 = aug_ref[0:LOG, 0:hid].astype(bf16)
     wd = aug_ref[LOG : 2 * LOG, 0:hid].astype(bf16)
-    b_out_0 = b_out_ref[0, 0]
-    b_out_1 = b_out_ref[0, 1]
+    b_out_0 = jnp.broadcast_to(b_out_ref[0:1, 0:1], (nx, ny))
+    b_out_1 = jnp.broadcast_to(b_out_ref[0:1, 1:2], (nx, ny))
 
     grad_ref[...] = jnp.zeros(grad_ref.shape, f32)
 
@@ -160,14 +182,15 @@
     def set_row(z, row, value):
         fd_ref[pl.ds(pl.multiple_of(z * (nx * TILE), nx * TILE) + row, nx, stride=TILE), :] = value
 
-    def tile(z):
+    def tiles(z):
         base = pl.multiple_of(z * (nx * TILE), nx * TILE)
         block = fd_ref[pl.ds(base, nx * TILE), :].astype(bf16)
-        return jnp.concatenate([block[x * TILE : (x + 1) * TILE, :] for x in range(nx)], axis=1)
-
-    def put_log(ref, z, value):
-        for x in range(nx):
-            at = pl.multiple_of(z * (nx * LOG), nx * LOG) + x * LOG
+        rows_of = [block[x * TILE : (x + 1) * TILE, :] for x in range(nx)]
+        return [jnp.concatenate(rows_of[x : x + xw], axis=1) for x in range(0, nx, xw)]
+
+    def put_log(ref, z, chunk, value):
+        for x in range(xw):
+            at = pl.multiple_of(z * (nx * LOG), nx * LOG) + (chunk * xw + x) * LOG
             ref[pl.ds(at, LOG), :] = value[:, x * ny : (x + 1) * ny]
 
     def get_log(ref, z, row):
@@ -179,50 +202,82 @@
     def put_field(ref, z, value, which=0):
         ref[pl.ds(pl.multiple_of(z * nx, nx) + which * rows, nx), :] = value
 
-    def layers(fds):
-        h1 = [jnp.tanh(dot(w1, fd)).astype(bf16) for fd in fds]
-        h2 = [jnp.tanh(dot(w2, jnp.concatenate([h, fd], axis=0))).astype(bf16) for h, fd in zip(h1, fds)]
-        logits = [dot(w3, h) for h in h2]
-        return h1, h2, logits
+    def interleave(works, lag):
+        left = list(works)
+        step = 0
+        while any(w is not None for w in left):
+            for i, w in enumerate(left):
+                if w is not None and step >= i * lag:
+                    if next(w, "end") == "end":
+                        left[i] = None
+            step += 1
+
+    def layers(z, fds, ref, h1, h2):
+        n = len(fds)
+        for t in range(n + 2):
+            if t < n:
+                h1.append(jnp.tanh(dot(w1, fds[t])).astype(bf16))
+            if 0 <= t - 1 < n:
+                both = jnp.concatenate([h1[t - 1], fds[t - 1]], axis=0)
+                h2.append(jnp.tanh(dot(w2, both)).astype(bf16))
+            if 0 <= t - 2:
+                put_log(ref, z, t - 2, dot(w3, h2[t - 2]))
+            yield
 
     def through(d, h):
         wide_h = h.astype(f32)
         return (d * (1.0 - wide_h * wide_h)).astype(bf16)
 
-    def layers_back(fds, h1, h2, zs):
-        d2 = [through(dot(wo, fd), h) for fd, h in zip(fds, h2)]
-        d1 = [through(dot(wm, d), h) for d, h in zip(d2, h1)]
-        for z, d in zip(zs, d1):
-            put_log(lg_ref, z, dot(wd, d))
-        total = grad_ref[:, 0 : 3 * hid + TILE]
-        for i in range(len(zs)):
-            left = jnp.concatenate([fds[i], h1[i]], axis=0)
-            right = jnp.concatenate([d1[i], d2[i], h2[i], fds[i]], axis=0)
-            total = total + lax.dot_general(
-                left, right, (((1,), (1,)), ((), ())), preferred_element_type=f32
-            )
-        grad_ref[:, 0 : 3 * hid + TILE] = total
+    def layers_back(z, fds, h1, h2, lefts, rights):
+        n = len(fds)
+        d1, d2 = [], []
+        for t in range(n + 2):
+            if t < n:
+                d2.append(through(dot(wo, fds[t]), h2[t]))
+            if 0 <= t - 1 < n:
+                d1.append(through(dot(wm, d2[t - 1]), h1[t - 1]))
+            if 0 <= t - 2:
+                put_log(lg_ref, z, t - 2, dot(wd, d1[t - 2]))
+            yield
+        lefts += [jnp.concatenate([a, b], axis=0) for a, b in zip(fds, h1)]
+        rights += [jnp.concatenate(parts, axis=0) for parts in zip(d1, d2, h2, fds)]
+
+    def add_terms(lefts, rights):
+        grad_ref[:, 0 : 3 * hid + TILE] = grad_ref[:, 0 : 3 * hid + TILE] + lax.dot_general(
+            jnp.concatenate(lefts, axis=1),
+            jnp.concatenate(rights, axis=1),
+            (((1,), (1,)), ((), ())),
+            preferred_element_type=f32,
+        )
 
     ones = jnp.ones((nx, ny), f32)
     nil = jnp.zeros((nx, ny), f32)
 
     def start_body(step, _):
         zs = [step * zb + i for i in range(zb)]
+        for d in range(ndesc):
+            span = pl.ds(pl.multiple_of(step * (zb * nx), zb * nx), zb * nx)
+            lines = desc_ref[d, span, :].astype(f32)
+            for i, z in enumerate(zs):
+                set_row(z, d, lines[i * nx : (i + 1) * nx, :])
         for z in zs:
-            for d in range(ndesc):
-                set_row(z, d, desc_ref[d, z].astype(f32))
             set_row(z, row_s, field(s_ref, z))
             set_row(z, row_s + 1, field(f_ref, z))
             set_row(z, row_one, ones)
             set_row(z, row_d, nil)
             set_row(z, row_d + 1, nil)
             set_row(z, row_two, ones)
-        fds = [tile(z) for z in zs]
-        h1, h2, logits = layers(fds)
-        for z, a, b, c in zip(zs, h1, h2, logits):
-            h1_ref[z] = a
-            h2_ref[z] = b
-            put_log(lg0_ref, z, c)
+
+        def work(z):
+            fds = tiles(z)
+            h1, h2 = [], []
+            yield from layers(z, fds, lg0_ref, h1, h2)
+            for chunk in range(len(fds)):
+                lanes = slice(chunk * xw * ny, (chunk + 1) * xw * ny)
+                h1_ref[z, :, lanes] = h1[chunk]
+                h2_ref[z, :, lanes] = h2[chunk]
+
+        interleave([work(z) for z in zs], 3)
         return 0
 
     lax.fori_loop(0, nz // zb, start_body, 0)
@@ -240,8 +295,9 @@
 
     def later_body(step, _):
         zs = [step * zb + i for i in range(zb)]
-        diff = []
-        for z in zs:
+        lefts, rights = [], []
+
+        def work(z):
             h_sf = gates(get_log(lg0_ref, z, 0) + b_out_0)[0]
             a_sf = gates(get_log(lg0_ref, z, 1) + b_out_1)[0]
             solid, fluid, free = field(s_ref, z), field(f_ref, z), field(free_ref, z)
@@ -250,24 +306,22 @@
             fluid_1 = fluid + field(us_ref, z, 1) * lap(fluid, field(halo_ref, z, 1)) - swap
             set_row(z, row_s, solid_1)
             set_row(z, row_s + 1, fluid_1)
-            diff.append(fluid_1 - solid_1)
-        fds = [tile(z) for z in zs]
-        h1, h2, logits = layers(fds)
-        for z, c in zip(zs, logits):
-            put_log(lg_ref, z, c)
-        swing = []
-        for z, d in zip(zs, diff):
-            turn = field(free_ref, z) * (field(gs_ref, z) - field(gf_ref, z))
-            swing.append(logit_cots(z, d * turn, lg_ref) * turn)
-        fds = [tile(z) for z in zs]
-        layers_back(fds, h1, h2, zs)
-        for z, w in zip(zs, swing):
-            new_s = field(gs_ref, z) + lap(field(ps_ref, z), field(halo_ref, z, 2)) - w + get_log(lg_ref, z, 0)
-            new_f = field(gf_ref, z) + lap(field(ps_ref, z, 1), field(halo_ref, z, 3)) + w + get_log(lg_ref, z, 1)
+            yield
+            h1, h2 = [], []
+            yield from layers(z, tiles(z), lg_ref, h1, h2)
+            turn = free * (field(gs_ref, z) - field(gf_ref, z))
+            swing = logit_cots(z, (fluid_1 - solid_1) * turn, lg_ref) * turn
+            yield
+            yield from layers_back(z, tiles(z), h1, h2, lefts, rights)
+            new_s = field(gs_ref, z) + lap(field(ps_ref, z), field(halo_ref, z, 2)) - swing + get_log(lg_ref, z, 0)
+            new_f = field(gf_ref, z) + lap(field(ps_ref, z, 1), field(halo_ref, z, 3)) + swing + get_log(lg_ref, z, 1)
             put_field(g2_ref, z, new_s)
             put_field(g2_ref, z, new_f, 1)
             put_field(ps_ref, z, field(us_ref, z) * new_s)
             put_field(ps_ref, z, field(us_ref, z, 1) * new_f, 1)
+
+        interleave([work(z) for z in zs], 5)
+        add_terms(lefts, rights)
         return 0
 
     lax.fori_loop(0, nz // zb, later_body, 0)
@@ -279,18 +333,24 @@
 
     def first_body(step, _):
         zs = [step * zb + i for i in range(zb)]
-        swing = []
-        for z in zs:
+        lefts, rights = [], []
+
+        def work(z):
             solid, fluid = field(s_ref, z), field(f_ref, z)
             set_row(z, row_s, solid)
             set_row(z, row_s + 1, fluid)
             turn = field(free_ref, z) * (field(g2_ref, z) - field(g2_ref, z, 1))
-            swing.append(logit_cots(z, (fluid - solid) * turn, lg0_ref) * turn)
-        fds = [tile(z) for z in zs]
-        layers_back(fds, [h1_ref[z] for z in zs], [h2_ref[z] for z in zs], zs)
-        for z, w in zip(zs, swing):
-            put_field(g2_ref, z, field(g2_ref, z) - w + get_log(lg_ref, z, 0))
-            put_field(g2_ref, z, field(g2_ref, z, 1) + w + get_log(lg_ref, z, 1), 1)
+            swing = logit_cots(z, (fluid - solid) * turn, lg0_ref) * turn
+            yield
+            parts = [slice(i * xw * ny, (i + 1) * xw * ny) for i in range(nx // xw)]
+            h1 = [h1_ref[z, :, lanes] for lanes in parts]
+            h2 = [h2_ref[z, :, lanes] for lanes in parts]
+            yield from layers_back(z, tiles(z), h1, h2, lefts, rights)
+            put_field(g2_ref, z, field(g2_ref, z) - swing + get_log(lg_ref, z, 0))
+            put_field(g2_ref, z, field(g2_ref, z, 1) + swing + get_log(lg_ref, z, 1), 1)
+
+        interleave([work(z) for z in zs], 3)
+        add_terms(lefts, rights)
         return 0
 
     lax.fori_loop(0, nz // zb, first_body, 0)
@@ -349,6 +409,12 @@
         return 0
 
     lax.fori_loop(0, nz, final_body, 0, unroll=zb)
+    stores = [
+        pltpu.make_async_copy(adj_s_ref, out_s_ref, out_sem.at[0]),
+        pltpu.make_async_copy(adj_f_ref, out_f_ref, out_sem.at[1]),
+    ]
+    for store in stores:
+        store.start()
 
     for copy in sends:
         copy.wait()
@@ -363,7 +429,30 @@
         copy.start()
     for copy in sends:
         copy.wait()
-    whole = jnp.concatenate([fin_ref[i] for i in range(ncol)], axis=0)
+    for i in range(ncol):
+        whole_ref[i * piece : (i + 1) * piece, :] = fin_ref[i]
+    for store in stores:
+        store.wait()
+
+
+def unpack(
+    ndesc, adj_s_ref, adj_f_ref, summed_ref, *refs
+):
+    targets, places, whole_ref, sem = refs[:8], refs[8:14], refs[14], refs[15]
+    fetch = pltpu.make_async_copy(summed_ref, whole_ref, sem.at[8])
+    fetch.start()
+    copies = [
+        pltpu.make_async_copy(source, target, sem.at[i])
+        for i, (source, target) in enumerate(zip((adj_s_ref, adj_f_ref) + places, targets))
+    ]
+    copies[0].start()
+    copies[1].start()
+    g_w_in_ref, g_b_in_ref, g_w_mid_ref, g_b_mid_ref, g_w_out_ref, g_b_out_ref = places
+    hid = g_w_mid_ref.shape[0]
+    half, wide_l = hid // 2, 2 * hid
+    row_one, row_d = ndesc + 2, ndesc + 3
+    fetch.wait()
+    whole = whole_ref[...]
     g_w_in_ref[...] = whole[0 : ndesc + 2, 0:hid]
     ones_row = whole[row_one : row_one + 1, :]
     g_b_in_ref[...] = ones_row[:, 0:hid]
@@ -378,6 +467,10 @@
     b1 = pltpu.roll(whole[at + 1 : at + 2, :], wide_l - one_lane + 1, 1)
     first_lane = lax.broadcasted_iota(jnp.int32, (1, wide_l), 1) == 0
     g_b_out_ref[...] = jnp.where(first_lane, b0, b1)[:, 0:2]
+    for copy in copies[2:]:
+        copy.start()
+    for copy in copies:
+        copy.wait()
 
 
 def solution(mesh):
@@ -396,17 +489,23 @@
         piece = 8 * -(-used // (8 * ncol))
         flat = lambda a: a.reshape(rows, ny)
         vmem = pl.BlockSpec(memory_space=pltpu.VMEM)
-        smem = pl.BlockSpec(memory_space=pltpu.SMEM)
+        hbm = pl.BlockSpec(memory_space=pltpu.HBM)
         sds = jax.ShapeDtypeStruct
-        outs = pl.pallas_call(
+        fetched = (
+            flat(fixed_mask), flat(material), solid_cond.reshape(1, -1), fluid_cond.reshape(1, -1),
+            flat(solid_cot), flat(fluid_cot), flat(solid_temp), flat(fluid_temp),
+            b_in.reshape(1, hid), b_mid.reshape(1, hid), w_mid, b_out.reshape(1, 2),
+            descriptors.reshape(ndesc, rows, ny),
+        )
+        held = pl.pallas_call(
             functools.partial(kernel, ngrp, ncol, scale, zb),
-            out_shape=(
-                sds((rows, ny), f32), sds((rows, ny), f32), sds((feat, hid), f32), sds((1, hid), f32),
-                sds((hid, hid), f32), sds((1, hid), f32), sds((2, hid), f32), sds((1, 2), f32),
-            ),
-            in_specs=[vmem] * 5 + [smem] * 2 + [vmem] * 5 + [smem] + [vmem] * 2,
-            out_specs=(vmem,) * 8,
-            scratch_shapes=[
+            out_shape=(sds((rows, ny), f32), sds((rows, ny), f32), sds((ncol * piece, 2 * hid), f32)),
+            in_specs=[vmem] * 2 + [hbm] * FETCHED,
+            out_specs=(hbm, hbm, vmem),
+            scratch_shapes=[pltpu.VMEM((rows, ny), f32), pltpu.VMEM((rows, ny), f32), pltpu.SemaphoreType.DMA((2,))]
+            + [pltpu.VMEM(a.shape, a.dtype) for a in fetched]
+            + [
+                pltpu.SemaphoreType.DMA((FETCHED,)),
                 pltpu.VMEM((128, 128), f32),
                 pltpu.VMEM((rows * TILE, ny), f32),
                 pltpu.VMEM((nz, hid, nx * ny), bf16),
@@ -443,14 +542,24 @@
                 pltpu.SemaphoreType.DMA((ncol - 1,)),
             ],
             compiler_params=pltpu.CompilerParams(
-                collective_id=0, has_side_effects=True, vmem_limit_bytes=48 * 1024 * 1024
+                collective_id=0, has_side_effects=True, vmem_limit_bytes=64 * 1024 * 1024
             ),
             name="wick_adjoint",
-        )(
-            descriptors, flat(solid_temp), flat(fluid_temp), flat(material), flat(fixed_mask),
-            solid_cond, fluid_cond, w_in, b_in.reshape(1, hid), w_mid, b_mid.reshape(1, hid),
-            w_out.T, b_out.reshape(1, 2), flat(solid_cot), flat(fluid_cot),
-        )
+        )(w_in, w_out.T, *fetched)
+        shapes = (
+            sds((rows, ny), f32), sds((rows, ny), f32), sds((feat, hid), f32), sds((1, hid), f32),
+            sds((hid, hid), f32), sds((1, hid), f32), sds((2, hid), f32), sds((1, 2), f32),
+        )
+        outs = pl.pallas_call(
+            functools.partial(unpack, ndesc),
+            out_shape=shapes,
+            in_specs=[hbm] * 3,
+            out_specs=(hbm,) * 8,
+            scratch_shapes=[pltpu.VMEM(a.shape, a.dtype) for a in shapes[2:]]
+            + [pltpu.VMEM((ncol * piece, 2 * hid), f32), pltpu.SemaphoreType.DMA((9,))],
+            compiler_params=pltpu.CompilerParams(vmem_limit_bytes=64 * 1024 * 1024),
+            name="unpack",
+        )(*held)
         block = lambda a: a.reshape(nz, nx, ny)
         return (
             block(outs[0]), block(outs[1]), outs[2], outs[3].reshape(hid),

time: 58.6 us -> 87.4 us (1.49)
  Pallas kernels: 44.4 us -> 86.6 us
  local copies, waits for them, and re-layouts: 13.1 us -> 0 us
    pallas_call x1, Pallas kernels: 44.4 us -> 77.4 us  [shards(): pl.pallas_call(functools.partial(kernel, ngrp, ncol, scale, zb), out_shap...]
    unnamed x38 -> x0, local copies, waits for them, and re-layouts: 13.1 us -> none
    pallas_call x0 -> x1, Pallas kernels: none -> 9.14 us  [shards(): pl.pallas_call(functools.partial(unpack, ndesc), out_shape=shapes, in_spe...]
where the time goes in v2:
time: 87.4 us; the launch traced here: 87.2 us
  Pallas kernels  86.6 us (99%)
    pallas_call x1, Pallas kernels, shards(): pl.pallas_call(functools.partial(kernel, ngrp, ncol, scale, zb), out_shap...  77.4 us
    pallas_call x1, Pallas kernels, shards(): pl.pallas_call(functools.partial(unpack, ndesc), out_shape=shapes, in_spe...  9.14 us

profile of v2, /device:TPU:0, one launch (start us, length us, event | category | flops | bytes accessed | tf_op | source)
XLA Modules:
  0.0 87.2 jit_solution(5502455495613326756)
XLA Ops:
  0.6 77.4 %wick_adjoint.1 = (f32[256,128]{1,0:T(8,128)}, f32[256,128]{1,0:T(8,128)}, f32[64,128]{1,0:T(8,128)}) custom-call(bf16[12,64]{1,0:T(8,128)(2,1)} %w_in_ref.1, bf16[2,64]{1,0:T(2,128)(2,1)} %bitcast.26, s32[256,128]{1,0:T(8,128)} %bitcast.20, s32[256,128]{1,0:T(8,128)} %bitcast.21, f32[1,4]{1,0:T(1,128)} %bitcast.27, f32[1,4]{1,0:T(1,128)} %bitcast.28, ...), custom_call_target="tpu_custom_call" | custom-call | tf_op jit(solution)/shard_map/wick_adjoint/pallas_call | solution.py:500
  78.1 9.1 %unpack.1 = (f32[256,128]{1,0:T(8,128)}, f32[256,128]{1,0:T(8,128)}, f32[12,64]{1,0:T(8,128)}, f32[1,64]{1,0:T(1,128)}, f32[64,64]{1,0:T(8,128)}, /*index=5*/f32...) custom-call(f32[256,128]{1,0:T(8,128)} %get-tuple-element.19.adj_s_ref, f32[256,128]{1,0:T(8,128)} %get-tuple-element.20.adj_f_ref, ...), custom_call_target="tpu_custom_call" | custom-call | tf_op jit(solution)/shard_map/unpack/pallas_call | solution.py:553

commit v3 on v1

--- a/solution.py
+++ b/solution.py
@@ -15,6 +15,7 @@
 bf16 = jnp.bfloat16
 TILE = 16
 LOG = 8
+FETCHED = 13
 
 
 def gates(logit):
@@ -26,15 +27,31 @@
 
 def kernel(
     ngrp, ncol, scale, zb,
-    desc_ref, s_ref, f_ref, mat_ref, mask_ref, scond_ref, fcond_ref,
-    w_in_ref, b_in_ref, w_mid_ref, b_mid_ref, w_out_t_ref, b_out_ref, gs_ref, gf_ref,
-    adj_s_ref, adj_f_ref, g_w_in_ref, g_b_in_ref, g_w_mid_ref, g_b_mid_ref, g_w_out_ref, g_b_out_ref,
+    w_in_ref, w_out_t_ref, *refs,
+):
+    sources, rest = refs[:FETCHED], refs[FETCHED:]
+    (
+    out_s_ref, out_f_ref, whole_ref, adj_s_ref, adj_f_ref, out_sem,
+    mask_ref, mat_ref, scond_ref, fcond_ref, gs_ref, gf_ref, s_ref, f_ref,
+    b_in_ref, b_mid_ref, w_mid_ref, b_out_ref, desc_ref, in_sem,
     aug_ref, fd_ref, h1_ref, h2_ref, lg0_ref, lg_ref, free_ref, us_ref, ps_ref, g2_ref,
     halo_ref, grad_ref, xs_ref, xr_ref, ys_ref, yr_ref, xs2_ref, xr2_ref, ys2_ref, yr2_ref,
     acc_ref, part_ref, grp_ref, fin_ref,
     hs_sem, hr_sem, hs2_sem, hr2_sem, c_ssem, c_rsem, g_ssem, g_rsem, a_ssem, a_rsem,
-):
-    ndesc, nz, nx, ny = desc_ref.shape
+    ) = rest
+    held = (
+        mask_ref, mat_ref, scond_ref, fcond_ref, gs_ref, gf_ref, s_ref, f_ref,
+        b_in_ref, b_mid_ref, w_mid_ref, b_out_ref, desc_ref,
+    )
+    fetches = [
+        pltpu.make_async_copy(source, place, in_sem.at[i])
+        for i, (source, place) in enumerate(zip(sources, held))
+    ]
+    for fetch in fetches:
+        fetch.start()
+    ndesc, _, ny = desc_ref.shape
+    nz = xs_ref.shape[2]
+    nx = s_ref.shape[0] // nz
     hid = w_mid_ref.shape[0]
     rows = nz * nx
     cells = nx * ny
@@ -62,14 +79,16 @@
     xi = lax.broadcasted_iota(jnp.int32, (nx, ny), 0)
     yi = lax.broadcasted_iota(jnp.int32, (nx, ny), 1)
 
+    for fetch in fetches[:8]:
+        fetch.wait()
     mat = mat_ref[...]
     free = time_step * (1.0 - mask_ref[...].astype(f32))
     free_ref[...] = free
     sk = jnp.zeros((rows, ny), f32)
     fk = jnp.zeros((rows, ny), f32)
-    for kind in range(scond_ref.shape[0]):
-        sk = sk + jnp.where(mat == kind, scond_ref[kind], 0.0)
-        fk = fk + jnp.where(mat == kind, fcond_ref[kind], 0.0)
+    for kind in range(scond_ref.shape[1]):
+        sk = sk + jnp.where(mat == kind, scond_ref[0:1, kind : kind + 1], 0.0)
+        fk = fk + jnp.where(mat == kind, fcond_ref[0:1, kind : kind + 1], 0.0)
     us_ref[0:rows, :] = sk * free
     us_ref[rows : 2 * rows, :] = fk * free
     ps_ref[0:rows, :] = us_ref[0:rows, :] * gs_ref[...]
@@ -122,6 +141,8 @@
     for copy in first:
         copy.start()
 
+    for fetch in fetches[8:]:
+        fetch.wait()
     wide = aug_ref.shape[1]
 
     def split(b):
@@ -149,8 +170,8 @@
     aug_ref[LOG : LOG + 2, 0:hid] = w_in[ndesc : ndesc + 2, :]
     w3 = aug_ref[0:LOG, 0:hid].astype(bf16)
     wd = aug_ref[LOG : 2 * LOG, 0:hid].astype(bf16)
-    b_out_0 = b_out_ref[0, 0]
-    b_out_1 = b_out_ref[0, 1]
+    b_out_0 = jnp.broadcast_to(b_out_ref[0:1, 0:1], (nx, ny))
+    b_out_1 = jnp.broadcast_to(b_out_ref[0:1, 1:2], (nx, ny))
 
     grad_ref[...] = jnp.zeros(grad_ref.shape, f32)
 
@@ -208,9 +229,12 @@
 
     def start_body(step, _):
         zs = [step * zb + i for i in range(zb)]
+        for d in range(ndesc):
+            span = pl.ds(pl.multiple_of(step * (zb * nx), zb * nx), zb * nx)
+            lines = desc_ref[d, span, :].astype(f32)
+            for i, z in enumerate(zs):
+                set_row(z, d, lines[i * nx : (i + 1) * nx, :])
         for z in zs:
-            for d in range(ndesc):
-                set_row(z, d, desc_ref[d, z].astype(f32))
             set_row(z, row_s, field(s_ref, z))
             set_row(z, row_s + 1, field(f_ref, z))
             set_row(z, row_one, ones)
@@ -349,6 +373,12 @@
         return 0
 
     lax.fori_loop(0, nz, final_body, 0, unroll=zb)
+    stores = [
+        pltpu.make_async_copy(adj_s_ref, out_s_ref, out_sem.at[0]),
+        pltpu.make_async_copy(adj_f_ref, out_f_ref, out_sem.at[1]),
+    ]
+    for store in stores:
+        store.start()
 
     for copy in sends:
         copy.wait()
@@ -363,7 +393,33 @@
         copy.start()
     for copy in sends:
         copy.wait()
-    whole = jnp.concatenate([fin_ref[i] for i in range(ncol)], axis=0)
+    for i in range(ncol):
+        whole_ref[i * piece : (i + 1) * piece, :] = fin_ref[i]
+    for store in stores:
+        store.wait()
+
+
+def unpack(
+    ndesc, adj_s_ref, adj_f_ref, summed_ref, *refs
+):
+    targets, places, held, in_sem, sem = refs[:8], refs[8:16], refs[16], refs[17], refs[18]
+    sources = (summed_ref, adj_s_ref, adj_f_ref)
+    fetches = [
+        pltpu.make_async_copy(source, place, in_sem.at[i])
+        for i, (source, place) in enumerate(zip(sources, (held, places[0], places[1])))
+    ]
+    for fetch in fetches:
+        fetch.start()
+    copies = [
+        pltpu.make_async_copy(place, target, sem.at[i])
+        for i, (place, target) in enumerate(zip(places, targets))
+    ]
+    fetches[0].wait()
+    whole = held[...]
+    g_w_in_ref, g_b_in_ref, g_w_mid_ref, g_b_mid_ref, g_w_out_ref, g_b_out_ref = places[2:]
+    hid = g_w_mid_ref.shape[0]
+    half, wide_l = hid // 2, 2 * hid
+    row_one, row_d = ndesc + 2, ndesc + 3
     g_w_in_ref[...] = whole[0 : ndesc + 2, 0:hid]
     ones_row = whole[row_one : row_one + 1, :]
     g_b_in_ref[...] = ones_row[:, 0:hid]
@@ -378,6 +434,13 @@
     b1 = pltpu.roll(whole[at + 1 : at + 2, :], wide_l - one_lane + 1, 1)
     first_lane = lax.broadcasted_iota(jnp.int32, (1, wide_l), 1) == 0
     g_b_out_ref[...] = jnp.where(first_lane, b0, b1)[:, 0:2]
+    for copy in copies[2:]:
+        copy.start()
+    for i in range(2):
+        fetches[i + 1].wait()
+        copies[i].start()
+    for copy in copies:
+        copy.wait()
 
 
 def solution(mesh):
@@ -396,17 +459,23 @@
         piece = 8 * -(-used // (8 * ncol))
         flat = lambda a: a.reshape(rows, ny)
         vmem = pl.BlockSpec(memory_space=pltpu.VMEM)
-        smem = pl.BlockSpec(memory_space=pltpu.SMEM)
+        hbm = pl.BlockSpec(memory_space=pltpu.HBM)
         sds = jax.ShapeDtypeStruct
-        outs = pl.pallas_call(
+        fetched = (
+            flat(fixed_mask), flat(material), solid_cond.reshape(1, -1), fluid_cond.reshape(1, -1),
+            flat(solid_cot), flat(fluid_cot), flat(solid_temp), flat(fluid_temp),
+            b_in.reshape(1, hid), b_mid.reshape(1, hid), w_mid, b_out.reshape(1, 2),
+            descriptors.reshape(ndesc, rows, ny),
+        )
+        held = pl.pallas_call(
             functools.partial(kernel, ngrp, ncol, scale, zb),
-            out_shape=(
-                sds((rows, ny), f32), sds((rows, ny), f32), sds((feat, hid), f32), sds((1, hid), f32),
-                sds((hid, hid), f32), sds((1, hid), f32), sds((2, hid), f32), sds((1, 2), f32),
-            ),
-            in_specs=[vmem] * 5 + [smem] * 2 + [vmem] * 5 + [smem] + [vmem] * 2,
-            out_specs=(vmem,) * 8,
-            scratch_shapes=[
+            out_shape=(sds((rows, ny), f32), sds((rows, ny), f32), sds((ncol * piece, 2 * hid), f32)),
+            in_specs=[vmem] * 2 + [hbm] * FETCHED,
+            out_specs=(hbm, hbm, vmem),
+            scratch_shapes=[pltpu.VMEM((rows, ny), f32), pltpu.VMEM((rows, ny), f32), pltpu.SemaphoreType.DMA((2,))]
+            + [pltpu.VMEM(a.shape, a.dtype) for a in fetched]
+            + [
+                pltpu.SemaphoreType.DMA((FETCHED,)),
                 pltpu.VMEM((128, 128), f32),
                 pltpu.VMEM((rows * TILE, ny), f32),
                 pltpu.VMEM((nz, hid, nx * ny), bf16),
@@ -443,14 +512,28 @@
                 pltpu.SemaphoreType.DMA((ncol - 1,)),
             ],
             compiler_params=pltpu.CompilerParams(
-                collective_id=0, has_side_effects=True, vmem_limit_bytes=48 * 1024 * 1024
+                collective_id=0, has_side_effects=True, vmem_limit_bytes=64 * 1024 * 1024
             ),
             name="wick_adjoint",
-        )(
-            descriptors, flat(solid_temp), flat(fluid_temp), flat(material), flat(fixed_mask),
-            solid_cond, fluid_cond, w_in, b_in.reshape(1, hid), w_mid, b_mid.reshape(1, hid),
-            w_out.T, b_out.reshape(1, 2), flat(solid_cot), flat(fluid_cot),
-        )
+        )(w_in, w_out.T, *fetched)
+        shapes = (
+            sds((rows, ny), f32), sds((rows, ny), f32), sds((feat, hid), f32), sds((1, hid), f32),
+            sds((hid, hid), f32), sds((1, hid), f32), sds((2, hid), f32), sds((1, 2), f32),
+        )
+        outs = pl.pallas_call(
+            functools.partial(unpack, ndesc),
+            out_shape=shapes,
+            in_specs=[hbm] * 3,
+            out_specs=(hbm,) * 8,
+            scratch_shapes=[pltpu.VMEM(a.shape, a.dtype) for a in shapes]
+            + [
+                pltpu.VMEM((ncol * piece, 2 * hid), f32),
+                pltpu.SemaphoreType.DMA((3,)),
+                pltpu.SemaphoreType.DMA((8,)),
+            ],
+            compiler_params=pltpu.CompilerParams(vmem_limit_bytes=64 * 1024 * 1024),
+            name="unpack",
+        )(*held)
         block = lambda a: a.reshape(nz, nx, ny)
         return (
             block(outs[0]), block(outs[1]), outs[2], outs[3].reshape(hid),

time: 58.6 us -> 47.7 us (0.81)
  local copies, waits for them, and re-layouts: 13.1 us -> 0 us
  Pallas kernels: 44.4 us -> 46.9 us
    unnamed x38 -> x0, local copies, waits for them, and re-layouts: 13.1 us -> none
    pallas_call x0 -> x1, Pallas kernels: none -> 1.75 us  [shards(): pl.pallas_call(functools.partial(unpack, ndesc), out_shape=shapes, in_spe...]
    pallas_call x1, Pallas kernels: 44.4 us -> 45.1 us  [shards(): pl.pallas_call(functools.partial(kernel, ngrp, ncol, scale, zb), out_shap...]
where the time goes in v3:
time: 47.7 us; the launch traced here: 47.5 us
  Pallas kernels  46.9 us (98%)
  between operations  0.65 us (1%)
    pallas_call x1, Pallas kernels, shards(): pl.pallas_call(functools.partial(kernel, ngrp, ncol, scale, zb), out_shap...  45.1 us
    pallas_call x1, Pallas kernels, shards(): pl.pallas_call(functools.partial(unpack, ndesc), out_shape=shapes, in_spe...  1.75 us

profile of v3, /device:TPU:0, one launch (start us, length us, event | category | flops | bytes accessed | tf_op | source)
XLA Modules:
  0.0 47.5 jit_solution(11758786114204424168)
XLA Ops:
  0.6 45.1 %wick_adjoint.1 = (f32[256,128]{1,0:T(8,128)}, f32[256,128]{1,0:T(8,128)}, f32[64,128]{1,0:T(8,128)}) custom-call(bf16[12,64]{1,0:T(8,128)(2,1)} %w_in_ref.1, bf16[2,64]{1,0:T(2,128)(2,1)} %bitcast.26, s32[256,128]{1,0:T(8,128)} %bitcast.20, s32[256,128]{1,0:T(8,128)} %bitcast.21, f32[1,4]{1,0:T(1,128)} %bitcast.27, f32[1,4]{1,0:T(1,128)} %bitcast.28, ...), custom_call_target="tpu_custom_call" | custom-call | tf_op jit(solution)/shard_map/wick_adjoint/pallas_call | solution.py:470
  45.8 1.8 %unpack.1 = (f32[256,128]{1,0:T(8,128)}, f32[256,128]{1,0:T(8,128)}, f32[12,64]{1,0:T(8,128)}, f32[1,64]{1,0:T(1,128)}, f32[64,64]{1,0:T(8,128)}, /*index=5*/f32...) custom-call(f32[256,128]{1,0:T(8,128)} %get-tuple-element.19.adj_s_ref, f32[256,128]{1,0:T(8,128)} %get-tuple-element.20.adj_f_ref, ...), custom_call_target="tpu_custom_call" | custom-call | tf_op jit(solution)/shard_map/unpack/pallas_call | solution.py:523

commit v4 on v3

--- a/solution.py
+++ b/solution.py
@@ -54,7 +54,6 @@
     nx = s_ref.shape[0] // nz
     hid = w_mid_ref.shape[0]
     rows = nz * nx
-    cells = nx * ny
     row_s, row_one, row_d, row_two = ndesc, ndesc + 2, ndesc + 3, ndesc + 5
     me_g = lax.axis_index("grp")
     me_c = lax.axis_index("col")
@@ -200,29 +199,34 @@
     def put_field(ref, z, value, which=0):
         ref[pl.ds(pl.multiple_of(z * nx, nx) + which * rows, nx), :] = value
 
-    def layers(fds):
-        h1 = [jnp.tanh(dot(w1, fd)).astype(bf16) for fd in fds]
-        h2 = [jnp.tanh(dot(w2, jnp.concatenate([h, fd], axis=0))).astype(bf16) for h, fd in zip(h1, fds)]
-        logits = [dot(w3, h) for h in h2]
-        return h1, h2, logits
+    cells = nx * ny
+
+    def beside(values):
+        return jnp.concatenate(values, axis=1)
+
+    def layer_of(value, i):
+        return value[:, i * cells : (i + 1) * cells]
+
+    def layers(fd):
+        h1 = jnp.tanh(dot(w1, fd)).astype(bf16)
+        h2 = jnp.tanh(dot(w2, jnp.concatenate([h1, fd], axis=0))).astype(bf16)
+        return h1, h2, dot(w3, h2)
 
     def through(d, h):
         wide_h = h.astype(f32)
         return (d * (1.0 - wide_h * wide_h)).astype(bf16)
 
-    def layers_back(fds, h1, h2, zs):
-        d2 = [through(dot(wo, fd), h) for fd, h in zip(fds, h2)]
-        d1 = [through(dot(wm, d), h) for d, h in zip(d2, h1)]
-        for z, d in zip(zs, d1):
-            put_log(lg_ref, z, dot(wd, d))
-        total = grad_ref[:, 0 : 3 * hid + TILE]
-        for i in range(len(zs)):
-            left = jnp.concatenate([fds[i], h1[i]], axis=0)
-            right = jnp.concatenate([d1[i], d2[i], h2[i], fds[i]], axis=0)
-            total = total + lax.dot_general(
-                left, right, (((1,), (1,)), ((), ())), preferred_element_type=f32
-            )
-        grad_ref[:, 0 : 3 * hid + TILE] = total
+    def layers_back(fd, h1, h2, zs):
+        d2 = through(dot(wo, fd), h2)
+        d1 = through(dot(wm, d2), h1)
+        d_temps = dot(wd, d1)
+        for i, z in enumerate(zs):
+            put_log(lg_ref, z, layer_of(d_temps, i))
+        left = jnp.concatenate([fd, h1], axis=0)
+        right = jnp.concatenate([d1, d2, h2, fd], axis=0)
+        grad_ref[:, 0 : 3 * hid + TILE] = grad_ref[:, 0 : 3 * hid + TILE] + lax.dot_general(
+            left, right, (((1,), (1,)), ((), ())), preferred_element_type=f32
+        )
 
     ones = jnp.ones((nx, ny), f32)
     nil = jnp.zeros((nx, ny), f32)
@@ -241,12 +245,11 @@
             set_row(z, row_d, nil)
             set_row(z, row_d + 1, nil)
             set_row(z, row_two, ones)
-        fds = [tile(z) for z in zs]
-        h1, h2, logits = layers(fds)
-        for z, a, b, c in zip(zs, h1, h2, logits):
-            h1_ref[z] = a
-            h2_ref[z] = b
-            put_log(lg0_ref, z, c)
+        h1, h2, logits = layers(beside([tile(z) for z in zs]))
+        h1_ref[step] = h1
+        h2_ref[step] = h2
+        for i, z in enumerate(zs):
+            put_log(lg0_ref, z, layer_of(logits, i))
         return 0
 
     lax.fori_loop(0, nz // zb, start_body, 0)
@@ -275,16 +278,14 @@
             set_row(z, row_s, solid_1)
             set_row(z, row_s + 1, fluid_1)
             diff.append(fluid_1 - solid_1)
-        fds = [tile(z) for z in zs]
-        h1, h2, logits = layers(fds)
-        for z, c in zip(zs, logits):
-            put_log(lg_ref, z, c)
+        h1, h2, logits = layers(beside([tile(z) for z in zs]))
+        for i, z in enumerate(zs):
+            put_log(lg_ref, z, layer_of(logits, i))
         swing = []
         for z, d in zip(zs, diff):
             turn = field(free_ref, z) * (field(gs_ref, z) - field(gf_ref, z))
             swing.append(logit_cots(z, d * turn, lg_ref) * turn)
-        fds = [tile(z) for z in zs]
-        layers_back(fds, h1, h2, zs)
+        layers_back(beside([tile(z) for z in zs]), h1, h2, zs)
         for z, w in zip(zs, swing):
             new_s = field(gs_ref, z) + lap(field(ps_ref, z), field(halo_ref, z, 2)) - w + get_log(lg_ref, z, 0)
             new_f = field(gf_ref, z) + lap(field(ps_ref, z, 1), field(halo_ref, z, 3)) + w + get_log(lg_ref, z, 1)
@@ -310,8 +311,7 @@
             set_row(z, row_s + 1, fluid)
             turn = field(free_ref, z) * (field(g2_ref, z) - field(g2_ref, z, 1))
             swing.append(logit_cots(z, (fluid - solid) * turn, lg0_ref) * turn)
-        fds = [tile(z) for z in zs]
-        layers_back(fds, [h1_ref[z] for z in zs], [h2_ref[z] for z in zs], zs)
+        layers_back(beside([tile(z) for z in zs]), h1_ref[step], h2_ref[step], zs)
         for z, w in zip(zs, swing):
             put_field(g2_ref, z, field(g2_ref, z) - w + get_log(lg_ref, z, 0))
             put_field(g2_ref, z, field(g2_ref, z, 1) + w + get_log(lg_ref, z, 1), 1)
@@ -478,8 +478,8 @@
                 pltpu.SemaphoreType.DMA((FETCHED,)),
                 pltpu.VMEM((128, 128), f32),
                 pltpu.VMEM((rows * TILE, ny), f32),
-                pltpu.VMEM((nz, hid, nx * ny), bf16),
-                pltpu.VMEM((nz, hid, nx * ny), bf16),
+                pltpu.VMEM((nz // zb, hid, zb * nx * ny), bf16),
+                pltpu.VMEM((nz // zb, hid, zb * nx * ny), bf16),
                 pltpu.VMEM((rows * LOG, ny), f32),
                 pltpu.VMEM((rows * LOG, ny), f32),
                 pltpu.VMEM((rows, ny), f32),

time: 47.7 us -> 47.8 us (level)
  no operation moved by 1% of the time
where the time goes in v4:
time: 47.8 us; the launch traced here: 47.6 us
  Pallas kernels  46.9 us (98%)
  between operations  0.65 us (1%)
    pallas_call x1, Pallas kernels, shards(): pl.pallas_call(functools.partial(kernel, ngrp, ncol, scale, zb), out_shap...  45.2 us
    pallas_call x1, Pallas kernels, shards(): pl.pallas_call(functools.partial(unpack, ndesc), out_shape=shapes, in_spe...  1.75 us

profile of v4, /device:TPU:0, one launch (start us, length us, event | category | flops | bytes accessed | tf_op | source)
XLA Modules:
  0.0 47.6 jit_solution(18413319107367251450)
XLA Ops:
  0.6 45.2 %wick_adjoint.1 = (f32[256,128]{1,0:T(8,128)}, f32[256,128]{1,0:T(8,128)}, f32[64,128]{1,0:T(8,128)}) custom-call(bf16[12,64]{1,0:T(8,128)(2,1)} %w_in_ref.1, bf16[2,64]{1,0:T(2,128)(2,1)} %bitcast.26, s32[256,128]{1,0:T(8,128)} %bitcast.20, s32[256,128]{1,0:T(8,128)} %bitcast.21, f32[1,4]{1,0:T(1,128)} %bitcast.27, f32[1,4]{1,0:T(1,128)} %bitcast.28, ...), custom_call_target="tpu_custom_call" | custom-call | tf_op jit(solution)/shard_map/wick_adjoint/pallas_call | solution.py:470
  45.8 1.8 %unpack.1 = (f32[256,128]{1,0:T(8,128)}, f32[256,128]{1,0:T(8,128)}, f32[12,64]{1,0:T(8,128)}, f32[1,64]{1,0:T(1,128)}, f32[64,64]{1,0:T(8,128)}, /*index=5*/f32...) custom-call(f32[256,128]{1,0:T(8,128)} %get-tuple-element.19.adj_s_ref, f32[256,128]{1,0:T(8,128)} %get-tuple-element.20.adj_f_ref, ...), custom_call_target="tpu_custom_call" | custom-call | tf_op jit(solution)/shard_map/unpack/pallas_call | solution.py:523
